TPU v7x, 512 devices: a whole 4x4x16 slice. The times are simulated.
512 devices in a mesh: dp: 4 (over x), row: 8 (over y, core), col: 16 (over z).
Axes of the slice: x: 4, y: 4, z: 16, core: 2. Of those that a mesh axis runs over, the one named last changes fastest.
Arguments:
- tokens: bfloat16 [2048, 6144], P(('dp', 'col'), 'row'), may hold values from -6 to 6
- weight_up: bfloat16 [6144, 24576], P('row', 'col'), may hold values from -0.078125 to 0.078125
- d_hidden: bfloat16 [2048, 24576], P(('dp', 'row'), 'col'), may hold values from -0.796875 to 0.796875
Outputs:
- d_tokens: bfloat16 [2048, 6144], P(('dp', 'col'), 'row')
- d_weight: bfloat16 [6144, 24576], P('row', 'col')
All inputs are finite; a program needn't handle non-finite values.
Results may differ from a plain program's by a relative error of at most 0.027.
Values may be sent and summed in bfloat16 or wider, within the bound.
No kernel may reach another device: no remote copies, remote signals or barrier semaphores. Data moves between devices by JAX's collectives and lax.ppermute only.
A program may use at most 64 MiB of HBM per device.

v0:
```python
import jax
import jax.numpy as jnp
from jax import lax
from jax.sharding import PartitionSpec as P


def gelu_back(pre, cot):
    value, pullback = jax.vjp(lambda v: jax.nn.gelu(v, approximate=True), pre)
    return pullback(cot.astype(jnp.float32))[0].astype(jnp.bfloat16)


def per_device(tokens, weight_up, d_hidden):
    panel = lax.all_gather(tokens, "col", axis=0, tiled=True)
    rows_in = panel
    pre = lax.psum_scatter(
        jnp.dot(rows_in, weight_up, preferred_element_type=jnp.float32).astype(jnp.bfloat16),
        "row",
        scatter_dimension=0,
        tiled=True,
    ).astype(jnp.float32)
    grad_local = gelu_back(pre, d_hidden)
    grad_all = lax.all_gather(grad_local, "row", axis=0, tiled=True)
    rows_in = grad_all
    d_tokens = lax.psum_scatter(
        lax.dot_general(
            rows_in, weight_up, (((1,), (1,)), ((), ())), preferred_element_type=jnp.float32
        ).astype(jnp.bfloat16),
        "col",
        scatter_dimension=0,
        tiled=True,
    )
    local_grad = lax.dot_general(
        panel, grad_all, (((0,), (0,)), ((), ())), preferred_element_type=jnp.float32
    )
    d_weight = lax.psum(local_grad.astype(jnp.bfloat16), "dp")
    return (d_tokens, d_weight)


def solution(mesh):
    placed = (P(("dp", "col"), "row"), P("row", "col"), P(("dp", "row"), "col"))
    return jax.shard_map(
        per_device,
        mesh=mesh,
        in_specs=placed,
        out_specs=(P(("dp", "col"), "row"), P("row", "col")),
        check_vma=False,
    )
```

profile of v0, /device:TPU:2, one launch (start us, length us, event | category | flops | bytes accessed | tf_op | source)
XLA Modules:
  0.0 282.8 jit_solution(4789410179036924260)
XLA Ops:
  7.2 0.0 copy-start
  7.2 0.0 reduce-scatter.3.cloned.1.call-start
  7.2 40.5 %all_gather.6 = bf16[512,768]{1,0:T(8,128)(2,1)S(1)} all-gather(bf16[32,768]{1,0:T(8,128)(2,1)} %param.3), channel_id=1, replica_groups=mesh['dp'=4,'row'=8,'col'=16] {'col'}, dimensions={0}, use_global_device_ids=true | all-gather | bytes 835584 | tf_op jit(solution)/shard_map/all_gather | solution.py:13
  47.8 0.0 copy-done
  47.8 0.0 copy-start.1
  47.8 2.5 convolution_convert_fusion.1
  50.3 0.0 reduce-scatter.3.cloned.1.call-update
  50.3 0.0 all-gather.2.cloned.1.call-start
  50.4 36.3 %reduce-scatter.3.cloned.1.call-done = bf16[64,1536]{1,0:T(8,128)(2,1)} async-done(((bf16[512,1536]{1,0:T(8,128)(2,1)}), bf16[64,1536]{1,0:T(8,128)(2,1)}) %reduce-scatter.3.cloned.1.call-update) | async-done | bytes 196624 | tf_op jit(solution)/shard_map/reduce_scatter | solution.py:15
  86.7 0.0 copy-done.1
  86.7 1.9 fusion.4
  88.6 0.0 all-gather.2.cloned.1.call-update
  88.6 0.0 all-reduce.2.cloned.1.call-start
  88.7 31.7 %all-gather.2.cloned.1.call-done = bf16[512,1536]{1,0:T(8,128)(2,1)} async-done(((bf16[64,1536]{1,0:T(8,128)(2,1)}), bf16[512,1536]{1,0:T(8,128)(2,1)}) %all-gather.2.cloned.1.call-update) | async-done | bytes 1572880 | tf_op jit(solution)/shard_map/all_gather | solution.py:22
  120.3 4.2 %fusion = bf16[768,1536]{0,1:T(8,128)(2,1)} fusion(bf16[512,1536]{1,0:T(8,128)(2,1)} %all-gather.2.cloned.1.call-done, bf16[512,768]{1,0:T(8,128)(2,1)S(1)} %all_gather.6), kind=kOutput, calls=%fused_computation.1 | convolution fusion | flops 1209139200 | bytes 4718592 | tf_op jit(solution)/shard_map/dot_general | solution.py:32
  124.6 0.0 all-reduce.2.cloned.1.call-update
  124.6 0.0 reduce-scatter.5.cloned.1.call-start
  124.6 3.7 %convolution_convert_fusion.2 = bf16[512,768]{1,0:T(8,128)(2,1)} fusion(bf16[512,1536]{1,0:T(8,128)(2,1)} %all-gather.2.cloned.1.call-done, bf16[768,1536]{1,0:T(8,128)(2,1)S(1)} %copy-done), kind=kOutput, calls=%fused_computation.3 | convolution fusion | flops 1208352768 | bytes 4718592 | tf_op jit(solution)/shard_map/dot_general | solution.py:25
  128.3 0.0 reduce-scatter.5.cloned.1.call-update
  128.4 73.8 %all-reduce.2.cloned.1.call-done = bf16[768,1536]{0,1:T(8,128)(2,1)} async-done(((bf16[768,1536]{0,1:T(8,128)(2,1)}), bf16[768,1536]{0,1:T(8,128)(2,1)}) %all-reduce.2.cloned.1.call-update) | async-done | bytes 2359312 | tf_op jit(solution)/shard_map/psum | solution.py:35
  202.2 4.3 %copy.5 = bf16[768,1536]{1,0:T(8,128)(2,1)} copy(bf16[768,1536]{0,1:T(8,128)(2,1)} %all-reduce.2.cloned.1.call-done) | data formatting | bytes 4718592
  206.5 69.8 %reduce-scatter.5.cloned.1.call-done = bf16[32,768]{1,0:T(8,128)(2,1)} async-done(((bf16[512,768]{1,0:T(8,128)(2,1)}), bf16[32,768]{1,0:T(8,128)(2,1)}) %reduce-scatter.5.cloned.1.call-update) | async-done | bytes 49168 | tf_op jit(solution)/shard_map/reduce_scatter | solution.py:24
Async XLA Ops:
  7.2 40.6 %copy-start = (bf16[768,1536]{1,0:T(8,128)(2,1)S(1)}, bf16[768,1536]{1,0:T(8,128)(2,1)}, u32[]{:S(2)}) copy-start(bf16[768,1536]{1,0:T(8,128)(2,1)} %param.4) | copy-start | bytes 7077892
  7.2 79.5 %reduce-scatter.3.cloned.1.call-start = ((), (), s32[]{:S(2)}) async-start(), calls=%async_computation.2 | async-start | bytes 1769472 | tf_op jit(solution)/shard_map/reduce_scatter | solution.py:15
  47.8 38.9 %copy-start.1 = (bf16[64,1536]{1,0:T(8,128)(2,1)S(1)}, bf16[64,1536]{1,0:T(8,128)(2,1)}, u32[]{:S(2)}) copy-start(bf16[64,1536]{1,0:T(8,128)(2,1)} %param.5) | copy-start | bytes 589828
  50.3 70.0 %all-gather.2.cloned.1.call-start = ((), (), s32[]{:S(2)}) async-start(), calls=%async_computation.3 | async-start | bytes 1769472 | tf_op jit(solution)/shard_map/all_gather | solution.py:22
  88.6 113.6 %all-reduce.2.cloned.1.call-start = ((), (), s32[]{:S(2)}) async-start(), calls=%async_computation.5 | async-start | bytes 4718592 | tf_op jit(solution)/shard_map/psum | solution.py:35
  124.6 151.7 %reduce-scatter.5.cloned.1.call-start = ((), (), s32[]{:S(2)}) async-start(), calls=%async_computation.4 | async-start | bytes 835584 | tf_op jit(solution)/shard_map/reduce_scatter | solution.py:24
Sparse Core Ops, SparseCore 0:
  50.5 36.1 reduce-scatter.2
  89.4 30.8 all-gather.1
  124.7 77.4 all-reduce.1
  205.4 70.7 reduce-scatter.4
where the time goes:
time: 283 us
  waiting for transfers between devices  212 us (75%)
  blocking collectives  40.5 us (14%)
  between operations  13.8 us (5%)
  matrix products  10.5 us (4%)
  local copies, waits for them, and re-layouts  4.28 us (2%)
    psum x1, waiting for transfers between devices, per_device(): d_weight = lax.psum(local_grad.astype(jnp.bfloat16), 'dp')  73.8 us
    reduce_scatter x1, waiting for transfers between devices, per_device(): lax.psum_scatter(lax.dot_general(rows_in, weight_up, (((1,), (1,)), ((),...  69.8 us
    all_gather x1, blocking collectives, per_device(): panel = lax.all_gather(tokens, 'col', axis=0, tiled=True)  40.5 us
    reduce_scatter x1, waiting for transfers between devices, per_device(): lax.psum_scatter(jnp.dot(rows_in, weight_up, preferred_element_type=jnp.f...  36.3 us
    all_gather x1, waiting for transfers between devices, per_device(): grad_all = lax.all_gather(grad_local, 'row', axis=0, tiled=True)  31.7 us
  transfers between devices with their start and end apart: 4, of which 4 were waited for; matrix products, arithmetic and copies ran while one was open for 3% of the time, Pallas kernels for 0%

commit v1 on v0

v1 whole, which is shorter than its diff:
```python
import functools

import jax
import jax.numpy as jnp
from jax import lax
from jax.experimental import pallas as pl
from jax.experimental.pallas import tpu as pltpu
from jax.sharding import PartitionSpec as P

F32 = jnp.float32
BF16 = jnp.bfloat16
VMEM_LIMIT = 24 * 1024 * 1024


def gelu_back(pre, cot):
    value, pullback = jax.vjp(lambda v: jax.nn.gelu(v, approximate=True), pre)
    return pullback(cot.astype(F32))[0].astype(BF16)


def shift(n, step):
    return [(i, (i + step) % n) for i in range(n)]


def tokens_kernel(where, own, other, w, plus, minus, across, keep, rows):
    core, k = where[0], where[1]
    n_y, per_row, width = own.shape
    half = per_row // 2
    block = n_y * half
    for i, step in enumerate((1, 3, 2, 0)):
        cls = lax.rem(k + step, 4)
        at = pl.ds(pl.multiple_of(lax.rem(cls, 2) * half, half), half)

        @pl.when(cls // 2 == core)
        def _():
            rows[pl.ds(i * block, block), :] = own[:, at, :].reshape(block, width)

        @pl.when(cls // 2 != core)
        def _():
            rows[pl.ds(i * block, block), :] = other[:, at, :].reshape(block, width)

    step = 256
    for n in range(w.shape[0] // step):
        cols = pl.ds(n * step, step)
        out = lax.dot_general(
            rows[...], w[cols, :], (((1,), (1,)), ((), ())), preferred_element_type=F32
        )
        plus[:, cols] = out[:block].astype(BF16)
        minus[:, cols] = out[block : 2 * block].astype(BF16)
        across[:, cols] = out[2 * block : 3 * block].astype(BF16)
        keep[:, cols] = out[3 * block :]


def tokens_parts(where, own, other, w):
    n_y, per_row, width = own.shape
    block, depth = n_y * per_row // 2, w.shape[0]
    vmem = pl.BlockSpec(memory_space=pltpu.VMEM)
    return pl.pallas_call(
        tokens_kernel,
        out_shape=[jax.ShapeDtypeStruct((block, depth), t) for t in (BF16, BF16, BF16, F32)],
        in_specs=[pl.BlockSpec(memory_space=pltpu.SMEM), vmem, vmem, vmem],
        out_specs=[vmem] * 4,
        scratch_shapes=[pltpu.VMEM((4 * block, width), BF16)],
        compiler_params=pltpu.CompilerParams(vmem_limit_bytes=VMEM_LIMIT),
        cost_estimate=pl.CostEstimate(
            flops=8 * block * width * depth, bytes_accessed=6 * 1024 * 1024, transcendentals=0
        ),
        name="tokens_parts",
    )(where, own, other, w)


def weight_kernel(which, has_add, where, t_all, own, up, far_a, far_b, down, *rest):
    out = rest[-1]
    n_dp = t_all.shape[0]
    dp = where[2]
    far = jnp.concatenate([far_a[...], far_b[...]], axis=0)
    total = None
    for step, g in ((0, own[...]), (1, up[...]), (2, far), (3, down[...])):
        t = t_all[step, which]
        part = lax.dot_general(t, g, (((0,), (0,)), ((), ())), preferred_element_type=F32)
        total = part if total is None else total + part
    if has_add:
        total = total + rest[0][...].astype(F32)
    out[...] = total.astype(BF16)


def weight_part(where, t_all, own, up, far_a, far_b, down, which, add=None):
    n_dp, _, tok, depth = t_all.shape
    width = own.shape[1]
    step = 512
    cut = lambda a: pl.BlockSpec((a.shape[0], step), lambda n: (0, n))
    operands = [own, up, far_a, far_b, down] + ([] if add is None else [add])
    return pl.pallas_call(
        functools.partial(weight_kernel, which, add is not None),
        grid=(width // step,),
        out_shape=jax.ShapeDtypeStruct((depth, width), BF16),
        in_specs=[
            pl.BlockSpec(memory_space=pltpu.SMEM),
            pl.BlockSpec(t_all.shape, lambda n: (0, 0, 0, 0)),
            *[cut(a) for a in operands],
        ],
        out_specs=pl.BlockSpec((depth, step), lambda n: (0, n)),
        compiler_params=pltpu.CompilerParams(vmem_limit_bytes=VMEM_LIMIT),
        cost_estimate=pl.CostEstimate(
            flops=2 * n_dp * tok * width * depth, bytes_accessed=8 * 1024 * 1024, transcendentals=0
        ),
        name="weight_part",
    )(where, t_all, *operands)


def per_device(tokens, weight_up, d_hidden):
    n_dp, n_row, n_col = lax.axis_size("dp"), lax.axis_size("row"), lax.axis_size("col")
    n_y = n_row // 2
    depth, width = weight_up.shape
    core = lax.axis_index("row") % 2
    col = lax.axis_index("col")
    other_core = [(i, i ^ 1) for i in range(n_row)]
    y_groups = [[2 * y + c for y in range(n_y)] for c in range(2)]
    where = jnp.stack([core, col % 4, lax.axis_index("dp")]).astype(jnp.int32)

    w_other = lax.ppermute(weight_up, "row", other_core)
    panel = lax.all_gather(tokens, "col", axis=0, tiled=True)
    per_row = panel.shape[0] // n_row
    split = panel.reshape(n_y, 2, per_row, depth)
    mine = lax.dynamic_index_in_dim(split, core, 1, keepdims=False).reshape(-1, depth)
    theirs = lax.dynamic_index_in_dim(split, 1 - core, 1, keepdims=False).reshape(-1, depth)
    swapped = lax.ppermute(theirs, "row", other_core)
    pair = jnp.stack([mine, swapped])
    t_up = lax.ppermute(pair, "dp", shift(n_dp, 1))
    t_down = lax.ppermute(pair, "dp", shift(n_dp, -1))

    chip = jnp.dot(mine, weight_up, preferred_element_type=F32)
    chip = chip + jnp.dot(swapped, w_other, preferred_element_type=F32)
    parts = lax.all_to_all(
        chip.astype(BF16), "row", 0, 0, tiled=True, axis_index_groups=y_groups
    )
    pre = parts.reshape(n_y, per_row, width).astype(F32).sum(0)
    grad = gelu_back(pre, d_hidden)

    own = lax.all_gather(grad, "row", axis=0, tiled=True, axis_index_groups=y_groups)
    other = lax.ppermute(own, "row", other_core)
    up = lax.ppermute(own, "dp", shift(n_dp, 1))
    down = lax.ppermute(own, "dp", shift(n_dp, -1))

    plus, minus, across, keep = tokens_parts(
        where, own.reshape(n_y, per_row, width), other.reshape(n_y, per_row, width), weight_up
    )
    plus = lax.ppermute(plus, "col", shift(n_col, 1))
    minus = lax.ppermute(minus, "col", shift(n_col, -1))
    across = lax.ppermute(across, "col", [(i, i ^ 2) for i in range(n_col)])
    quad = (keep + plus.astype(F32) + minus.astype(F32) + across.astype(F32)).astype(BF16)

    up, down, quad = lax.optimization_barrier((up, down, quad))
    t_up, t_down = lax.optimization_barrier((t_up, t_down))
    t_far = jnp.stack([
        lax.ppermute(t_up[0], "dp", shift(n_dp, 1)),
        lax.ppermute(t_down[1], "dp", shift(n_dp, -1)),
    ])
    t_all = jnp.stack([pair, t_up, t_far, t_down])
    halves = own.shape[0] // 2
    far_a = lax.ppermute(up[:halves], "dp", shift(n_dp, 1))
    far_b = lax.ppermute(down[halves:], "dp", shift(n_dp, -1))

    col_groups = [[c + 4 * q for q in range(n_col // 4)] for c in range(4)]
    parts = lax.all_to_all(quad, "col", 0, 0, tiled=True, axis_index_groups=col_groups)

    g = (own, up, far_a, far_b, down)
    away = lax.ppermute(weight_part(where, t_all, *g, 1), "row", other_core)
    here = weight_part(where, t_all, *g, 0)
    parts, here = lax.optimization_barrier((parts, here))
    d_tokens = parts.reshape(n_col // 4, -1, depth).astype(F32).sum(0).astype(BF16)
    d_weight = (here.astype(F32) + away.astype(F32)).astype(BF16)
    return d_tokens, d_weight


def solution(mesh):
    placed = (P(("dp", "col"), "row"), P("row", "col"), P(("dp", "row"), "col"))
    return jax.shard_map(
        per_device,
        mesh=mesh,
        in_specs=placed,
        out_specs=(P(("dp", "col"), "row"), P("row", "col")),
        check_vma=False,
    )
```

time: 283 us -> 171 us (0.60)
  the two profiles are of different devices: /device:TPU:2 before, /device:TPU:1 now
where the time goes in v1:
time: 171 us; the launch traced here: 169 us
  starting transfers between devices  70.2 us (41%)
  blocking collectives  40.1 us (23%)
  waiting for transfers between devices  22 us (13%)
  other arithmetic  12.1 us (7%)
  Pallas kernels  11.3 us (7%)
  local copies, waits for them, and re-layouts  8.02 us (5%)
  matrix products  4.25 us (2%)
    all_gather x1, blocking collectives, per_device(): panel = lax.all_gather(tokens, 'col', axis=0, tiled=True)  28.4 us
    all_gather x1, blocking collectives, per_device(): lax.all_gather(grad, 'row', axis=0, tiled=True, axis_index_groups=y_groups)  11.7 us
    ppermute x1, starting transfers between devices, per_device(): w_other = lax.ppermute(weight_up, 'row', other_core)  8.92 us
    pallas_call x2, Pallas kernels, weight_part(): pl.pallas_call(functools.partial(weight_kernel, which, add is not None),...  8.59 us
    ppermute x1, starting transfers between devices, per_device(): swapped = lax.ppermute(theirs, 'row', other_core)  8.3 us
    all_to_all x1, starting transfers between devices, per_device(): lax.all_to_all(quad, 'col', 0, 0, tiled=True, axis_index_groups=col_groups)  6.71 us
    ppermute x1, waiting for transfers between devices, per_device(): far_a = lax.ppermute(up[:halves], 'dp', shift(n_dp, 1))  6.68 us
    ppermute x1, starting transfers between devices, per_device(): other = lax.ppermute(own, 'row', other_core)  5.87 us
  transfers between devices with their start and end apart: 17, of which 6 were waited for; matrix products, arithmetic and copies ran while one was open for 6% of the time, Pallas kernels for 4%

profile of v1, /device:TPU:1, one launch (start us, length us, event | category | flops | bytes accessed | tf_op | source)
XLA Modules:
  0.0 169.0 jit_solution(710537109957887566)
XLA Ops:
  0.6 8.9 %collective-permute-start.1 = (bf16[768,1536]{1,0:T(8,128)(2,1)}, bf16[768,1536]{1,0:T(8,128)(2,1)}, u32[]{:S(2)}, u32[]{:S(2)}) collective-permute-start(bf16[768,1536]{1,0:T(8,128)(2,1)} %w.1), channel_id=1, source_target_pairs={{0,16},{16,0},{32,48},{48,32},{64,80},{80,64},{96,112},{112,96},{1... | collective-permute-start | bytes 7077896 | tf_op jit(solution)/shard_map/ppermute | solution.py:120
  9.6 28.4 %all_gather.6 = bf16[512,768]{1,0:T(8,128)(2,1)S(1)} all-gather(bf16[32,768]{1,0:T(8,128)(2,1)} %param.3), channel_id=1, replica_groups=mesh['dp'=4,'row'=8,'col'=16] {'col'}, dimensions={0}, use_global_device_ids=true | all-gather | bytes 835584 | tf_op jit(solution)/shard_map/all_gather | solution.py:121
  38.0 8.3 %collective-permute-start = (bf16[256,768]{1,0:T(8,128)(2,1)S(1)}, bf16[256,768]{1,0:T(8,128)(2,1)S(1)}, u32[]{:S(2)}, u32[]{:S(2)}) collective-permute-start(bf16[256,768]{1,0:T(8,128)(2,1)S(1)} %bitcast.43), channel_id=1, source_target_pairs={{0,16},{16,0},{32,48},{48,32},{64,80},{80,64},{96,112},{112,96},{1... | collective-permute-start | bytes 1179656 | tf_op jit(solution)/shard_map/ppermute | solution.py:126
  47.6 3.5 %fusion = bf16[256,1536]{1,0:T(8,128)(2,1)} fusion(f32[256,1536]{1,0:T(8,128)S(1)} %fusion.12, bf16[256,768]{1,0:T(8,128)(2,1)S(1)} %collective-permute-done, bf16[768,1536]{1,0:T(8,128)(2,1)} %collective-permute-done.1), kind=kOutput, calls=%fused_computation.3 | convolution fusion | flops 604766208 | bytes 5111808 | tf_op jit(solution)/shard_map/dot_general | solution.py:132
  51.1 4.2 %all-to-all-start = ((bf16[4,64,1536]{2,1,0:T(8,128)(2,1)}), bf16[4,64,1536]{2,1,0:T(8,128)(2,1)S(1)}, u32[]{:S(2)}, u32[]{:S(2)}) async-start(bf16[4,64,1536]{2,1,0:T(8,128)(2,1)} %bitcast.3), calls=%async_computation | async-start | bytes 1572864 | tf_op jit(solution)/shard_map/all_to_all | solution.py:133
  55.3 2.3 %fusion.11 = (bf16[1,2,256,768]{3,2,1,0:T(8,128)(2,1)}, bf16[2,256,768]{2,1,0:T(8,128)(2,1)}) fusion(bf16[1,256,768]{2,1,0:T(8,128)(2,1)} %bitcast.39, bf16[1,256,768]{2,1,0:T(8,128)(2,1)S(1)} %bitcast.37), kind=kLoop, calls=%fused_computation.27 | loop fusion | flops 393216 | bytes 2359296 | tf_op jit(solution)/shard_map/stack | solution.py:158
  57.6 3.1 %collective-permute-start.8 = (bf16[2,256,768]{2,1,0:T(8,128)(2,1)}, bf16[2,256,768]{2,1,0:T(8,128)(2,1)}, u32[]{:S(2)}, u32[]{:S(2)}) collective-permute-start(bf16[2,256,768]{2,1,0:T(8,128)(2,1)} %get-tuple-element.25), channel_id=1, source_target_pairs={{0,128},{128,256},{256,384},{384,0},{1,129},{129,257},{257,385},{3... | collective-permute-start | bytes 2359304 | tf_op jit(solution)/shard_map/ppermute | solution.py:128
  60.7 3.4 %collective-permute-start.9 = (bf16[2,256,768]{2,1,0:T(8,128)(2,1)}, bf16[2,256,768]{2,1,0:T(8,128)(2,1)}, u32[]{:S(2)}, u32[]{:S(2)}) collective-permute-start(bf16[2,256,768]{2,1,0:T(8,128)(2,1)} %get-tuple-element.25), channel_id=1, source_target_pairs={{0,384},{128,0},{256,128},{384,256},{1,385},{129,1},{257,129},{385... | collective-permute-start | bytes 2359304 | tf_op jit(solution)/shard_map/ppermute | solution.py:129
  64.1 3.0 %all-to-all-done = bf16[4,64,1536]{2,1,0:T(8,128)(2,1)S(1)} async-done(((bf16[4,64,1536]{2,1,0:T(8,128)(2,1)}), bf16[4,64,1536]{2,1,0:T(8,128)(2,1)S(1)}, u32[]{:S(2)}, u32[]{:S(2)}) %all-to-all-start) | async-done | bytes 786464 | tf_op jit(solution)/shard_map/all_to_all | solution.py:133
  68.4 11.7 %all_gather.7.own = bf16[256,1536]{1,0:T(8,128)(2,1)S(1)} all-gather(bf16[64,1536]{1,0:T(8,128)(2,1)S(1)} %fusion.3), channel_id=1, replica_groups={{0,32,64,96},{16,48,80,112},{1,33,65,97},{17,49,81,113},{2,34,66,98},{1..., dimensions={0}, use_global_device_ids=true | all-gather | bytes 983040 | tf_op jit(solution)/shard_map/all_gather | solution.py:139
  80.1 5.9 %collective-permute-start.4 = (bf16[256,1536]{1,0:T(8,128)(2,1)S(1)}, bf16[256,1536]{1,0:T(8,128)(2,1)}, u32[]{:S(2)}, u32[]{:S(2)}) collective-permute-start(bf16[256,1536]{1,0:T(8,128)(2,1)S(1)} %all_gather.7.own), channel_id=1, source_target_pairs={{0,16},{16,0},{32,48},{48,32},{64,80},{80,64},{96,112},{112,96},{1... | collective-permute-start | bytes 2359304 | tf_op jit(solution)/shard_map/ppermute | solution.py:140
  86.1 3.2 %collective-permute-start.2 = (bf16[256,1536]{1,0:T(8,128)(2,1)S(1)}, bf16[256,1536]{1,0:T(8,128)(2,1)S(1)}, u32[]{:S(2)}, u32[]{:S(2)}) collective-permute-start(bf16[256,1536]{1,0:T(8,128)(2,1)S(1)} %all_gather.7.own), channel_id=1, source_target_pairs={{0,128},{128,256},{256,384},{384,0},{1,129},{129,257},{257,385},{3... | collective-permute-start | bytes 2359304 | tf_op jit(solution)/shard_map/ppermute | solution.py:141
  89.3 3.3 %collective-permute-start.3 = (bf16[256,1536]{1,0:T(8,128)(2,1)S(1)}, bf16[256,1536]{1,0:T(8,128)(2,1)S(1)}, u32[]{:S(2)}, u32[]{:S(2)}) collective-permute-start(bf16[256,1536]{1,0:T(8,128)(2,1)S(1)} %all_gather.7.own), channel_id=1, source_target_pairs={{0,384},{128,0},{256,128},{384,256},{1,385},{129,1},{257,129},{385... | collective-permute-start | bytes 2359304 | tf_op jit(solution)/shard_map/ppermute | solution.py:142
  93.6 2.7 %tokens_parts.1 = (bf16[128,768]{1,0:T(8,128)(2,1)S(1)}, bf16[128,768]{1,0:T(8,128)(2,1)S(1)}, bf16[128,768]{1,0:T(8,128)(2,1)S(1)}, f32[128,768]{1,0:T(8,128)S(1)}) custom-call(s32[3]{0:T(128)S(1)} %pad_add_fusion.where, bf16[4,64,1536]{2,1,0:T(8,128)(2,1)S(1)} %bitcast.35, bf16[4,64,1536]{2,1,0:T(8,128)(2,1)} %bitcast.8.other, bf16[768,1536]{1,0:T(8,128)(2,1)S(1)} %copy-done.1), custom_call_target="tpu_custom_call" | custom-call | flops 1207959552 | bytes 6291456 | tf_op jit(solution)/shard_map/tokens_parts/pallas_call | solution.py:57
  96.4 1.9 %collective-permute-start.7 = (bf16[128,768]{1,0:T(8,128)(2,1)S(1)}, bf16[128,768]{1,0:T(8,128)(2,1)S(1)}, u32[]{:S(2)}, u32[]{:S(2)}) collective-permute-start(bf16[128,768]{1,0:T(8,128)(2,1)S(1)} %get-tuple-element.16), channel_id=1, source_target_pairs={{0,2},{1,3},{2,0},{3,1},{4,6},{5,7},{6,4},{7,5},{8,10},{9,11},{10,... | collective-permute-start | bytes 589832 | tf_op jit(solution)/shard_map/ppermute | solution.py:149
  98.3 4.0 %collective-permute-start.6 = (bf16[128,768]{1,0:T(8,128)(2,1)S(1)}, bf16[128,768]{1,0:T(8,128)(2,1)S(1)}, u32[]{:S(2)}, u32[]{:S(2)}) collective-permute-start(bf16[128,768]{1,0:T(8,128)(2,1)S(1)} %get-tuple-element.15), channel_id=1, source_target_pairs={{0,15},{1,0},{2,1},{3,2},{4,3},{5,4},{6,5},{7,6},{8,7},{9,8},{10,9... | collective-permute-start | bytes 589832 | tf_op jit(solution)/shard_map/ppermute | solution.py:148
  102.2 1.9 %collective-permute-start.5 = (bf16[128,768]{1,0:T(8,128)(2,1)S(1)}, bf16[128,768]{1,0:T(8,128)(2,1)S(1)}, u32[]{:S(2)}, u32[]{:S(2)}) collective-permute-start(bf16[128,768]{1,0:T(8,128)(2,1)S(1)} %get-tuple-element.14), channel_id=1, source_target_pairs={{0,1},{1,2},{2,3},{3,4},{4,5},{5,6},{6,7},{7,8},{8,9},{9,10},{10,1... | collective-permute-start | bytes 589832 | tf_op jit(solution)/shard_map/ppermute | solution.py:147
  105.2 4.4 %collective-permute-done.7 = bf16[128,768]{1,0:T(8,128)(2,1)S(1)} collective-permute-done((bf16[128,768]{1,0:T(8,128)(2,1)S(1)}, bf16[128,768]{1,0:T(8,128)(2,1)S(1)}, u32[]{:S(2)}, u32[]{:S(2)}) %collective-permute-start.7) | collective-permute-done | bytes 196640 | tf_op jit(solution)/shard_map/ppermute | solution.py:149
  109.6 3.2 %collective-permute-start.11 = (bf16[256,768]{1,0:T(8,128)(2,1)S(1)}, bf16[256,768]{1,0:T(8,128)(2,1)S(1)}, u32[]{:S(2)}, u32[]{:S(2)}) collective-permute-start(bf16[256,768]{1,0:T(8,128)(2,1)S(1)} %slice_bitcast_fusion), channel_id=1, source_target_pairs={{0,384},{128,0},{256,128},{384,256},{1,385},{129,1},{257,129},{385... | collective-permute-start | bytes 1179656 | tf_op jit(solution)/shard_map/ppermute | solution.py:156
  112.8 2.1 %collective-permute-start.10 = (bf16[256,768]{1,0:T(8,128)(2,1)S(1)}, bf16[256,768]{1,0:T(8,128)(2,1)S(1)}, u32[]{:S(2)}, u32[]{:S(2)}) collective-permute-start(bf16[256,768]{1,0:T(8,128)(2,1)S(1)} %slice_bitcast_fusion.1), channel_id=1, source_target_pairs={{0,128},{128,256},{256,384},{384,0},{1,129},{129,257},{257,385},{3... | collective-permute-start | bytes 1179656 | tf_op jit(solution)/shard_map/ppermute | solution.py:155
  115.8 2.0 %collective-permute-start.12 = (bf16[128,1536]{1,0:T(8,128)(2,1)S(1)}, bf16[128,1536]{1,0:T(8,128)(2,1)S(1)}, u32[]{:S(2)}, u32[]{:S(2)}) collective-permute-start(bf16[128,1536]{1,0:T(8,128)(2,1)S(1)} %slice.14), channel_id=1, source_target_pairs={{0,128},{128,256},{256,384},{384,0},{1,129},{129,257},{257,385},{3... | collective-permute-start | bytes 1179656 | tf_op jit(solution)/shard_map/ppermute | solution.py:160
  117.8 4.5 %collective-permute-start.13 = (bf16[128,1536]{1,0:T(8,128)(2,1)S(1)}, bf16[128,1536]{1,0:T(8,128)(2,1)S(1)}, u32[]{:S(2)}, u32[]{:S(2)}) collective-permute-start(bf16[128,1536]{1,0:T(8,128)(2,1)S(1)} %slice.15), channel_id=1, source_target_pairs={{0,384},{128,0},{256,128},{384,256},{1,385},{129,1},{257,129},{385... | collective-permute-start | bytes 1179656 | tf_op jit(solution)/shard_map/ppermute | solution.py:161
  122.3 3.3 %collective-permute-done.10 = bf16[256,768]{1,0:T(8,128)(2,1)S(1)} collective-permute-done((bf16[256,768]{1,0:T(8,128)(2,1)S(1)}, bf16[256,768]{1,0:T(8,128)(2,1)S(1)}, u32[]{:S(2)}, u32[]{:S(2)}) %collective-permute-start.10) | collective-permute-done | bytes 393248 | tf_op jit(solution)/shard_map/ppermute | solution.py:155
  125.8 1.6 pad_maximum_fusion.t_all
  127.4 6.7 %collective-permute-done.12.far_a = bf16[128,1536]{1,0:T(8,128)(2,1)S(1)} collective-permute-done((bf16[128,1536]{1,0:T(8,128)(2,1)S(1)}, bf16[128,1536]{1,0:T(8,128)(2,1)S(1)}, u32[]{:S(2)}, u32[]{:S(2)}) %collective-permute-start.12) | collective-permute-done | bytes 393248 | tf_op jit(solution)/shard_map/ppermute | solution.py:160
  134.1 4.7 %weight_part.3 = bf16[768,1536]{1,0:T(8,128)(2,1)} custom-call(s32[3]{0:T(128)S(1)} %pad_add_fusion.where, bf16[4,2,256,768]{3,2,1,0:T(8,128)(2,1)S(1)} %pad_maximum_fusion.t_all, bf16[256,1536]{1,0:T(8,128)(2,1)S(1)} %copy-done.3, bf16[256,1536]{1,0:T(8,128)(2,1)S(1)} %collective-permute-done.2.up, bf16[128,1536]{1,0:T(8,128)(2,1)S(1)} %collective-permute-done.12.far_a, ...), custom_call_target="tpu_custom_call" | custom-call | flops 2415919104 | bytes 8388608 | tf_op jit(solution)/shard_map/weight_part/pallas_call | solution.py:92
  138.8 3.7 %collective-permute-start.14 = (bf16[768,1536]{1,0:T(8,128)(2,1)}, bf16[768,1536]{1,0:T(8,128)(2,1)}, u32[]{:S(2)}, u32[]{:S(2)}) collective-permute-start(bf16[768,1536]{1,0:T(8,128)(2,1)} %weight_part.3), channel_id=1, source_target_pairs={{0,16},{16,0},{32,48},{48,32},{64,80},{80,64},{96,112},{112,96},{1... | collective-permute-start | bytes 7077896 | tf_op jit(solution)/shard_map/ppermute | solution.py:167
  142.5 6.7 %all-to-all-start.1 = ((bf16[4,32,768]{2,1,0:T(8,128)(2,1)}), bf16[4,32,768]{2,1,0:T(8,128)(2,1)}, u32[]{:S(2)}, u32[]{:S(2)}) async-start(bf16[4,32,768]{2,1,0:T(8,128)(2,1)} %bitcast.40), calls=%async_computation.1 | async-start | bytes 393216 | tf_op jit(solution)/shard_map/all_to_all | solution.py:164
  153.6 3.9 %weight_part.2 = bf16[768,1536]{1,0:T(8,128)(2,1)S(1)} custom-call(s32[3]{0:T(128)S(1)} %pad_add_fusion.where, bf16[4,2,256,768]{3,2,1,0:T(8,128)(2,1)S(1)} %pad_maximum_fusion.t_all, bf16[256,1536]{1,0:T(8,128)(2,1)S(1)} %copy-done.4, bf16[256,1536]{1,0:T(8,128)(2,1)S(1)} %copy-done.6, bf16[128,1536]{1,0:T(8,128)(2,1)S(1)} %collective-permute-done.12.far_a, ...), custom_call_target="tpu_custom_call" | custom-call | flops 2415919104 | bytes 8388608 | tf_op jit(solution)/shard_map/weight_part/pallas_call | solution.py:92
  159.0 4.0 %all-to-all-done.1 = bf16[4,32,768]{2,1,0:T(8,128)(2,1)} async-done(((bf16[4,32,768]{2,1,0:T(8,128)(2,1)}), bf16[4,32,768]{2,1,0:T(8,128)(2,1)}, u32[]{:S(2)}, u32[]{:S(2)}) %all-to-all-start.1) | async-done | bytes 196640 | tf_op jit(solution)/shard_map/all_to_all | solution.py:164
  163.0 1.6 reduce_sum.22
  164.6 4.4 %add_convert_fusion = bf16[768,1536]{1,0:T(8,128)(2,1)} fusion(bf16[768,1536]{1,0:T(8,128)(2,1)} %collective-permute-done.14, bf16[768,1536]{1,0:T(8,128)(2,1)} %copy-done), kind=kLoop, calls=%fused_computation | loop fusion | flops 4718592 | bytes 7077888 | tf_op jit(solution)/shard_map/convert_element_type | solution.py:171
  (49 shorter events, 11.6 us)
Async XLA Ops:
  0.6 45.7 %copy-start.1 = (bf16[768,1536]{1,0:T(8,128)(2,1)S(1)}, bf16[768,1536]{1,0:T(8,128)(2,1)}, u32[]{:S(2)}) copy-start(bf16[768,1536]{1,0:T(8,128)(2,1)} %w.1) | copy-start | bytes 7077892
  0.6 47.0 %collective-permute-start.1 = (bf16[768,1536]{1,0:T(8,128)(2,1)}, bf16[768,1536]{1,0:T(8,128)(2,1)}, u32[]{:S(2)}, u32[]{:S(2)}) collective-permute-start(bf16[768,1536]{1,0:T(8,128)(2,1)} %w.1), channel_id=1, source_target_pairs={{0,16},{16,0},{32,48},{48,32},{64,80},{80,64},{96,112},{112,96},{1... | collective-permute-start | bytes 7077896 | tf_op jit(solution)/shard_map/ppermute | solution.py:120
  38.0 9.6 %collective-permute-start = (bf16[256,768]{1,0:T(8,128)(2,1)S(1)}, bf16[256,768]{1,0:T(8,128)(2,1)S(1)}, u32[]{:S(2)}, u32[]{:S(2)}) collective-permute-start(bf16[256,768]{1,0:T(8,128)(2,1)S(1)} %bitcast.43), channel_id=1, source_target_pairs={{0,16},{16,0},{32,48},{48,32},{64,80},{80,64},{96,112},{112,96},{1... | collective-permute-start | bytes 1179656 | tf_op jit(solution)/shard_map/ppermute | solution.py:126
  47.6 3.5 %copy-start.12 = (bf16[256,768]{1,0:T(8,128)(2,1)}, bf16[256,768]{1,0:T(8,128)(2,1)S(1)}, u32[]{:S(2)}) copy-start(bf16[256,768]{1,0:T(8,128)(2,1)S(1)} %collective-permute-done) | copy-start | bytes 1179652
  51.1 15.9 %all-to-all-start = ((bf16[4,64,1536]{2,1,0:T(8,128)(2,1)}), bf16[4,64,1536]{2,1,0:T(8,128)(2,1)S(1)}, u32[]{:S(2)}, u32[]{:S(2)}) async-start(bf16[4,64,1536]{2,1,0:T(8,128)(2,1)} %bitcast.3), calls=%async_computation | async-start | bytes 1572864 | tf_op jit(solution)/shard_map/all_to_all | solution.py:133
  57.6 28.5 %collective-permute-start.8 = (bf16[2,256,768]{2,1,0:T(8,128)(2,1)}, bf16[2,256,768]{2,1,0:T(8,128)(2,1)}, u32[]{:S(2)}, u32[]{:S(2)}) collective-permute-start(bf16[2,256,768]{2,1,0:T(8,128)(2,1)} %get-tuple-element.25), channel_id=1, source_target_pairs={{0,128},{128,256},{256,384},{384,0},{1,129},{129,257},{257,385},{3... | collective-permute-start | bytes 2359304 | tf_op jit(solution)/shard_map/ppermute | solution.py:128
  60.7 25.4 %collective-permute-start.9 = (bf16[2,256,768]{2,1,0:T(8,128)(2,1)}, bf16[2,256,768]{2,1,0:T(8,128)(2,1)}, u32[]{:S(2)}, u32[]{:S(2)}) collective-permute-start(bf16[2,256,768]{2,1,0:T(8,128)(2,1)} %get-tuple-element.25), channel_id=1, source_target_pairs={{0,384},{128,0},{256,128},{384,256},{1,385},{129,1},{257,129},{385... | collective-permute-start | bytes 2359304 | tf_op jit(solution)/shard_map/ppermute | solution.py:129
  80.1 16.3 %copy-start.2 = (bf16[256,1536]{1,0:T(8,128)(2,1)}, bf16[256,1536]{1,0:T(8,128)(2,1)S(1)}, u32[]{:S(2)}) copy-start(bf16[256,1536]{1,0:T(8,128)(2,1)S(1)} %all_gather.7.own) | copy-start | bytes 2359300
  80.1 13.5 %collective-permute-start.4 = (bf16[256,1536]{1,0:T(8,128)(2,1)S(1)}, bf16[256,1536]{1,0:T(8,128)(2,1)}, u32[]{:S(2)}, u32[]{:S(2)}) collective-permute-start(bf16[256,1536]{1,0:T(8,128)(2,1)S(1)} %all_gather.7.own), channel_id=1, source_target_pairs={{0,16},{16,0},{32,48},{48,32},{64,80},{80,64},{96,112},{112,96},{1... | collective-permute-start | bytes 2359304 | tf_op jit(solution)/shard_map/ppermute | solution.py:140
  86.1 29.7 %collective-permute-start.2 = (bf16[256,1536]{1,0:T(8,128)(2,1)S(1)}, bf16[256,1536]{1,0:T(8,128)(2,1)S(1)}, u32[]{:S(2)}, u32[]{:S(2)}) collective-permute-start(bf16[256,1536]{1,0:T(8,128)(2,1)S(1)} %all_gather.7.own), channel_id=1, source_target_pairs={{0,128},{128,256},{256,384},{384,0},{1,129},{129,257},{257,385},{3... | collective-permute-start | bytes 2359304 | tf_op jit(solution)/shard_map/ppermute | solution.py:141
  89.3 26.5 %collective-permute-start.3 = (bf16[256,1536]{1,0:T(8,128)(2,1)S(1)}, bf16[256,1536]{1,0:T(8,128)(2,1)S(1)}, u32[]{:S(2)}, u32[]{:S(2)}) collective-permute-start(bf16[256,1536]{1,0:T(8,128)(2,1)S(1)} %all_gather.7.own), channel_id=1, source_target_pairs={{0,384},{128,0},{256,128},{384,256},{1,385},{129,1},{257,129},{385... | collective-permute-start | bytes 2359304 | tf_op jit(solution)/shard_map/ppermute | solution.py:142
  96.4 13.3 %collective-permute-start.7 = (bf16[128,768]{1,0:T(8,128)(2,1)S(1)}, bf16[128,768]{1,0:T(8,128)(2,1)S(1)}, u32[]{:S(2)}, u32[]{:S(2)}) collective-permute-start(bf16[128,768]{1,0:T(8,128)(2,1)S(1)} %get-tuple-element.16), channel_id=1, source_target_pairs={{0,2},{1,3},{2,0},{3,1},{4,6},{5,7},{6,4},{7,5},{8,10},{9,11},{10,... | collective-permute-start | bytes 589832 | tf_op jit(solution)/shard_map/ppermute | solution.py:149
  98.3 14.5 %collective-permute-start.6 = (bf16[128,768]{1,0:T(8,128)(2,1)S(1)}, bf16[128,768]{1,0:T(8,128)(2,1)S(1)}, u32[]{:S(2)}, u32[]{:S(2)}) collective-permute-start(bf16[128,768]{1,0:T(8,128)(2,1)S(1)} %get-tuple-element.15), channel_id=1, source_target_pairs={{0,15},{1,0},{2,1},{3,2},{4,3},{5,4},{6,5},{7,6},{8,7},{9,8},{10,9... | collective-permute-start | bytes 589832 | tf_op jit(solution)/shard_map/ppermute | solution.py:148
  102.2 12.7 %collective-permute-start.5 = (bf16[128,768]{1,0:T(8,128)(2,1)S(1)}, bf16[128,768]{1,0:T(8,128)(2,1)S(1)}, u32[]{:S(2)}, u32[]{:S(2)}) collective-permute-start(bf16[128,768]{1,0:T(8,128)(2,1)S(1)} %get-tuple-element.14), channel_id=1, source_target_pairs={{0,1},{1,2},{2,3},{3,4},{4,5},{5,6},{6,7},{7,8},{8,9},{9,10},{10,1... | collective-permute-start | bytes 589832 | tf_op jit(solution)/shard_map/ppermute | solution.py:147
  105.2 20.6 %copy-start.11 = (bf16[1,2,256,768]{3,2,1,0:T(8,128)(2,1)S(1)}, bf16[1,2,256,768]{3,2,1,0:T(8,128)(2,1)}, u32[]{:S(2)}) copy-start(bf16[1,2,256,768]{3,2,1,0:T(8,128)(2,1)} %get-tuple-element.24) | copy-start | bytes 2359300
  109.6 12.7 %collective-permute-start.11 = (bf16[256,768]{1,0:T(8,128)(2,1)S(1)}, bf16[256,768]{1,0:T(8,128)(2,1)S(1)}, u32[]{:S(2)}, u32[]{:S(2)}) collective-permute-start(bf16[256,768]{1,0:T(8,128)(2,1)S(1)} %slice_bitcast_fusion), channel_id=1, source_target_pairs={{0,384},{128,0},{256,128},{384,256},{1,385},{129,1},{257,129},{385... | collective-permute-start | bytes 1179656 | tf_op jit(solution)/shard_map/ppermute | solution.py:156
  112.8 12.9 %collective-permute-start.10 = (bf16[256,768]{1,0:T(8,128)(2,1)S(1)}, bf16[256,768]{1,0:T(8,128)(2,1)S(1)}, u32[]{:S(2)}, u32[]{:S(2)}) collective-permute-start(bf16[256,768]{1,0:T(8,128)(2,1)S(1)} %slice_bitcast_fusion.1), channel_id=1, source_target_pairs={{0,128},{128,256},{256,384},{384,0},{1,129},{129,257},{257,385},{3... | collective-permute-start | bytes 1179656 | tf_op jit(solution)/shard_map/ppermute | solution.py:155
  115.7 18.4 %copy-start.5 = (bf16[256,1536]{1,0:T(8,128)(2,1)}, bf16[256,1536]{1,0:T(8,128)(2,1)S(1)}, u32[]{:S(2)}) copy-start(bf16[256,1536]{1,0:T(8,128)(2,1)S(1)} %collective-permute-done.2.up) | copy-start | bytes 2359300
  115.7 18.4 %copy-start.7 = (bf16[256,1536]{1,0:T(8,128)(2,1)}, bf16[256,1536]{1,0:T(8,128)(2,1)S(1)}, u32[]{:S(2)}) copy-start(bf16[256,1536]{1,0:T(8,128)(2,1)S(1)} %collective-permute-done.3.down) | copy-start | bytes 2359300
  115.8 18.3 %collective-permute-start.12 = (bf16[128,1536]{1,0:T(8,128)(2,1)S(1)}, bf16[128,1536]{1,0:T(8,128)(2,1)S(1)}, u32[]{:S(2)}, u32[]{:S(2)}) collective-permute-start(bf16[128,1536]{1,0:T(8,128)(2,1)S(1)} %slice.14), channel_id=1, source_target_pairs={{0,128},{128,256},{256,384},{384,0},{1,129},{129,257},{257,385},{3... | collective-permute-start | bytes 1179656 | tf_op jit(solution)/shard_map/ppermute | solution.py:160
  117.8 16.3 %collective-permute-start.13 = (bf16[128,1536]{1,0:T(8,128)(2,1)S(1)}, bf16[128,1536]{1,0:T(8,128)(2,1)S(1)}, u32[]{:S(2)}, u32[]{:S(2)}) collective-permute-start(bf16[128,1536]{1,0:T(8,128)(2,1)S(1)} %slice.15), channel_id=1, source_target_pairs={{0,384},{128,0},{256,128},{384,256},{1,385},{129,1},{257,129},{385... | collective-permute-start | bytes 1179656 | tf_op jit(solution)/shard_map/ppermute | solution.py:161
  125.8 8.4 %copy-start.3 = (bf16[256,1536]{1,0:T(8,128)(2,1)S(1)}, bf16[256,1536]{1,0:T(8,128)(2,1)}, u32[]{:S(2)}) copy-start(bf16[256,1536]{1,0:T(8,128)(2,1)} %copy-done.2) | copy-start | bytes 2359300
  134.1 4.7 %copy-start.9 = (bf16[128,1536]{1,0:T(8,128)(2,1)}, bf16[128,1536]{1,0:T(8,128)(2,1)S(1)}, u32[]{:S(2)}) copy-start(bf16[128,1536]{1,0:T(8,128)(2,1)S(1)} %collective-permute-done.13.far_b) | copy-start | bytes 1179652
  138.8 25.7 %collective-permute-start.14 = (bf16[768,1536]{1,0:T(8,128)(2,1)}, bf16[768,1536]{1,0:T(8,128)(2,1)}, u32[]{:S(2)}, u32[]{:S(2)}) collective-permute-start(bf16[768,1536]{1,0:T(8,128)(2,1)} %weight_part.3), channel_id=1, source_target_pairs={{0,16},{16,0},{32,48},{48,32},{64,80},{80,64},{96,112},{112,96},{1... | collective-permute-start | bytes 7077896 | tf_op jit(solution)/shard_map/ppermute | solution.py:167
  142.5 20.5 %all-to-all-start.1 = ((bf16[4,32,768]{2,1,0:T(8,128)(2,1)}), bf16[4,32,768]{2,1,0:T(8,128)(2,1)}, u32[]{:S(2)}, u32[]{:S(2)}) async-start(bf16[4,32,768]{2,1,0:T(8,128)(2,1)} %bitcast.40), calls=%async_computation.1 | async-start | bytes 393216 | tf_op jit(solution)/shard_map/all_to_all | solution.py:164
  149.2 1.1 copy-start.4
  150.4 1.1 copy-start.6
  151.5 1.1 copy-start.8
  152.6 1.0 copy-start.10
  157.5 1.4 copy-start

commit v2 on v1

v2 whole, which is shorter than its diff:
```python
import functools

import jax
import jax.numpy as jnp
from jax import lax
from jax.experimental import pallas as pl
from jax.experimental.pallas import tpu as pltpu
from jax.sharding import PartitionSpec as P

F32 = jnp.float32
BF16 = jnp.bfloat16
VMEM_LIMIT = 56 * 1024 * 1024
TOKENS_VMEM = 24 * 1024 * 1024


def gelu_back(pre, cot):
    value, pullback = jax.vjp(lambda v: jax.nn.gelu(v, approximate=True), pre)
    return pullback(cot.astype(F32))[0].astype(BF16)


def shift(n, step):
    return [(i, (i + step) % n) for i in range(n)]


together = lax.optimization_barrier


def tokens_kernel(where, own, other, w, plus, minus, across, keep, rows):
    core, k = where[0], where[1]
    n_y, per_row, width = own.shape
    half = per_row // 2
    block = n_y * half

    @pl.when(pl.program_id(0) == 0)
    def _():
        for i, step in enumerate((1, 3, 2, 0)):
            cls = lax.rem(k + step, 4)
            at = pl.ds(pl.multiple_of(lax.rem(cls, 2) * half, half), half)

            @pl.when(cls // 2 == core)
            def _():
                rows[pl.ds(i * block, block), :] = own[:, at, :].reshape(block, width)

            @pl.when(cls // 2 != core)
            def _():
                rows[pl.ds(i * block, block), :] = other[:, at, :].reshape(block, width)

    out = lax.dot_general(
        rows[...], w[...], (((1,), (1,)), ((), ())), preferred_element_type=F32
    )
    plus[...] = out[:block].astype(BF16)
    minus[...] = out[block : 2 * block].astype(BF16)
    across[...] = out[2 * block : 3 * block].astype(BF16)
    keep[...] = out[3 * block :]


def tokens_parts(where, own, other, w):
    n_y, per_row, width = own.shape
    block, depth = n_y * per_row // 2, w.shape[0]
    step = 256
    whole = pl.BlockSpec(own.shape, lambda n: (0, 0, 0))
    return pl.pallas_call(
        tokens_kernel,
        grid=(depth // step,),
        out_shape=[jax.ShapeDtypeStruct((block, depth), t) for t in (BF16, BF16, BF16, F32)],
        in_specs=[
            pl.BlockSpec(memory_space=pltpu.SMEM),
            whole,
            whole,
            pl.BlockSpec((step, width), lambda n: (n, 0)),
        ],
        out_specs=[pl.BlockSpec((block, step), lambda n: (0, n))] * 4,
        scratch_shapes=[pltpu.VMEM((4 * block, width), BF16)],
        compiler_params=pltpu.CompilerParams(vmem_limit_bytes=TOKENS_VMEM),
        cost_estimate=pl.CostEstimate(
            flops=8 * block * width * depth, bytes_accessed=6 * 1024 * 1024, transcendentals=0
        ),
        name="tokens_parts",
    )(where, own, other, w)


def weight_kernel(n, n_add, where, *refs):
    out, add, refs = refs[-1], refs[3 * n : -1], refs[: 3 * n]
    core = where[0]
    total = sum(r[...].astype(F32) for r in add) if n_add else None
    for i in range(n):
        t, mine, theirs = refs[3 * i : 3 * i + 3]
        depth = t.shape[-1]
        for half, g in ((core, mine), (1 - core, theirs)):
            part = lax.dot_general(
                t[:, half].reshape(g.shape[0], depth),
                g[...],
                (((0,), (0,)), ((), ())),
                preferred_element_type=F32,
            )
            total = part if total is None else total + part
    out[...] = total.astype(BF16)


def weight_part(where, terms, *adds):
    t, g = terms[0][0], terms[0][1]
    depth, width = t.shape[-1], g.shape[1]
    step = 512
    t_spec = pl.BlockSpec(t.shape, lambda n: (0, 0, 0, 0))
    g_spec = pl.BlockSpec((g.shape[0], step), lambda n: (0, n))
    out = pl.BlockSpec((depth, step), lambda n: (0, n))
    return pl.pallas_call(
        functools.partial(weight_kernel, len(terms), len(adds)),
        grid=(width // step,),
        out_shape=jax.ShapeDtypeStruct((depth, width), BF16),
        in_specs=[pl.BlockSpec(memory_space=pltpu.SMEM)]
        + [t_spec, g_spec, g_spec] * len(terms)
        + [out] * len(adds),
        out_specs=out,
        compiler_params=pltpu.CompilerParams(vmem_limit_bytes=VMEM_LIMIT),
        cost_estimate=pl.CostEstimate(
            flops=0,
            bytes_accessed=0,
            transcendentals=0,
        ),
        name="weight_part",
    )(where, *[a for term in terms for a in term], *adds)


def per_device(tokens, weight_up, d_hidden):
    n_dp, n_row, n_col = lax.axis_size("dp"), lax.axis_size("row"), lax.axis_size("col")
    n_y = n_row // 2
    depth, width = weight_up.shape
    core = lax.axis_index("row") % 2
    col = lax.axis_index("col")
    other_core = [(i, i ^ 1) for i in range(n_row)]
    y_groups = [[2 * y + c for y in range(n_y)] for c in range(2)]
    where = jnp.stack([core, col % 4, lax.axis_index("dp")]).astype(jnp.int32)

    panel = lax.all_gather(tokens, "col", axis=0, tiled=True)
    per_row = panel.shape[0] // n_row
    panel = panel.reshape(n_y, 2, per_row, depth)
    mine = lax.dynamic_index_in_dim(panel, core, 1, keepdims=False).reshape(-1, depth)
    theirs = lax.dynamic_index_in_dim(panel, 1 - core, 1, keepdims=False).reshape(-1, depth)

    got = lax.ppermute(
        jnp.dot(theirs, weight_up, preferred_element_type=F32).astype(BF16), "row", other_core
    )
    chip = jnp.dot(mine, weight_up, preferred_element_type=F32)
    chip = (chip + got.astype(F32)).astype(BF16)
    panel, chip = together((panel, chip))
    parts = lax.all_to_all(chip, "row", 0, 0, tiled=True, axis_index_groups=y_groups)

    t_up = lax.ppermute(panel, "dp", shift(n_dp, 1))
    t_down = lax.ppermute(panel, "dp", shift(n_dp, -1))

    pre = parts.reshape(n_y, per_row, width).astype(F32).sum(0)
    grad = gelu_back(pre, d_hidden)

    own = lax.all_gather(grad, "row", axis=0, tiled=True, axis_index_groups=y_groups)
    other = lax.ppermute(own, "row", other_core)
    up = lax.ppermute(own, "dp", shift(n_dp, 1))
    down = lax.ppermute(own, "dp", shift(n_dp, -1))

    other, t_up, t_down = together((other, t_up, t_down))

    plus, minus, across, keep = tokens_parts(
        where,
        own.reshape(n_y, per_row, width),
        other.reshape(n_y, per_row, width),
        weight_up,
    )
    plus = lax.ppermute(plus, "col", shift(n_col, 1))
    minus = lax.ppermute(minus, "col", shift(n_col, -1))
    across = lax.ppermute(across, "col", [(i, i ^ 2) for i in range(n_col)])

    up, down, plus, minus = together((up, down, plus, minus))
    far = lax.ppermute(down, "dp", shift(n_dp, -1))
    t_far = lax.ppermute(t_up, "dp", shift(n_dp, 1))
    up_other = lax.ppermute(up, "row", other_core)
    down_other = lax.ppermute(down, "row", other_core)

    quad = (keep + plus.astype(F32) + minus.astype(F32) + across.astype(F32)).astype(BF16)
    col_groups = [[c + 4 * q for q in range(n_col // 4)] for c in range(4)]
    parts = lax.all_to_all(quad, "col", 0, 0, tiled=True, axis_index_groups=col_groups)

    far_other = lax.ppermute(far, "row", other_core)
    d_weight = weight_part(
        where,
        [
            (panel, own, other),
            (t_up, up, up_other),
            (t_down, down, down_other),
            (t_far, far, far_other),
        ],
    )
    parts, d_weight = together((parts, d_weight))
    d_tokens = parts.reshape(n_col // 4, -1, depth).astype(F32).sum(0).astype(BF16)
    return d_tokens, d_weight


def solution(mesh):
    placed = (P(("dp", "col"), "row"), P("row", "col"), P(("dp", "row"), "col"))
    return jax.shard_map(
        per_device,
        mesh=mesh,
        in_specs=placed,
        out_specs=(P(("dp", "col"), "row"), P("row", "col")),
        check_vma=False,
    )
```

time: 171 us -> 156 us (0.912)
  other arithmetic: 12.1 us -> 1.89 us
  starting transfers between devices: 70.2 us -> 62 us
  blocking collectives: 40.1 us -> 46.1 us
  local copies, waits for them, and re-layouts: 8.02 us -> 2.91 us
  waiting for transfers between devices: 22 us -> 26.8 us
  matrix products: 4.25 us -> 2.44 us
    ppermute x9 -> x8, starting transfers between devices: 39.1 us -> 30.9 us  [the longest x1 9.64 us: per_device(): lax.ppermute(jnp.dot(theirs, weight_up, preferred_element_type=F32).astyp...]
    all_gather x1, blocking collectives: 28.4 us -> 34.3 us  [per_device(): panel = lax.all_gather(tokens, 'col', axis=0, tiled=True)]
    ppermute x1, waiting for transfers between devices: 0.01 us -> 5.11 us  [per_device(): up = lax.ppermute(own, 'dp', shift(n_dp, 1))]
    ppermute x1, waiting for transfers between devices: 4.43 us -> 0.01 us  [per_device(): across = lax.ppermute(across, 'col', [(i, i ^ 2) for i in range(n_col)])]
    convert_element_type x1 -> x0, other arithmetic: 4.39 us -> none  [per_device(): d_weight = (here.astype(F32) + away.astype(F32)).astype(BF16)]
    another operation x3 -> x0, other arithmetic: 3.98 us -> none  [per_device(): t_all = jnp.stack([pair, t_up, t_far, t_down])]
    ppermute x1, waiting for transfers between devices: 0.01 us -> 3.75 us  [per_device(): down = lax.ppermute(own, 'dp', shift(n_dp, -1))]
    unnamed x26 -> x18, local copies, waits for them, and re-layouts: 5.86 us -> 2.86 us
  transfers between devices with their start and end apart: 17 -> 16, of which waited for: 6 -> 6; matrix products, arithmetic and copies ran while one was open for 6% -> 1% of each run, Pallas kernels for 4% -> 8%
where the time goes in v2:
time: 156 us; the launch traced here: 155 us
  starting transfers between devices  62 us (40%)
  blocking collectives  46.1 us (30%)
  waiting for transfers between devices  26.8 us (17%)
  Pallas kernels  11.9 us (8%)
  local copies, waits for them, and re-layouts  2.91 us (2%)
  matrix products  2.44 us (2%)
  other arithmetic  1.89 us (1%)
    all_gather x1, blocking collectives, per_device(): panel = lax.all_gather(tokens, 'col', axis=0, tiled=True)  34.3 us
    all_gather x1, blocking collectives, per_device(): lax.all_gather(grad, 'row', axis=0, tiled=True, axis_index_groups=y_groups)  11.7 us
    ppermute x1, starting transfers between devices, per_device(): lax.ppermute(jnp.dot(theirs, weight_up, preferred_element_type=F32).astyp...  9.64 us
    pallas_call x1, Pallas kernels, weight_part(): pl.pallas_call(functools.partial(weight_kernel, len(terms), len(adds)), g...  9.27 us
    ppermute x1, waiting for transfers between devices, per_device(): far = lax.ppermute(down, 'dp', shift(n_dp, -1))  7.04 us
    all_to_all x1, starting transfers between devices, per_device(): lax.all_to_all(quad, 'col', 0, 0, tiled=True, axis_index_groups=col_groups)  6.24 us
    ppermute x1, starting transfers between devices, per_device(): other = lax.ppermute(own, 'row', other_core)  5.88 us
    all_to_all x1, waiting for transfers between devices, per_device(): lax.all_to_all(chip, 'row', 0, 0, tiled=True, axis_index_groups=y_groups)  5.39 us
  transfers between devices with their start and end apart: 16, of which 6 were waited for; matrix products, arithmetic and copies ran while one was open for 1% of the time, Pallas kernels for 8%

profile of v2, /device:TPU:1, one launch (start us, length us, event | category | flops | bytes accessed | tf_op | source)
XLA Modules:
  0.0 154.9 jit_solution(7961231455405486589)
XLA Ops:
  0.7 34.3 %all_gather.6 = bf16[512,768]{1,0:T(8,128)(2,1)S(1)} all-gather(bf16[32,768]{1,0:T(8,128)(2,1)} %param.3), channel_id=1, replica_groups=mesh['dp'=4,'row'=8,'col'=16] {'col'}, dimensions={0}, use_global_device_ids=true | all-gather | bytes 835584 | tf_op jit(solution)/shard_map/all_gather | solution.py:135
  35.0 0.8 convolution_convert_fusion
  35.8 9.6 %collective-permute-start = (bf16[256,1536]{1,0:T(8,128)(2,1)S(1)}, bf16[256,1536]{1,0:T(8,128)(2,1)S(1)}, u32[]{:S(2)}, u32[]{:S(2)}) collective-permute-start(bf16[256,1536]{1,0:T(8,128)(2,1)S(1)} %convolution_convert_fusion), channel_id=1, source_target_pairs={{0,16},{16,0},{32,48},{48,32},{64,80},{80,64},{96,112},{112,96},{1... | collective-permute-start | bytes 2359304 | tf_op jit(solution)/shard_map/ppermute | solution.py:141
  45.5 1.9 %collective-permute-done = bf16[256,1536]{1,0:T(8,128)(2,1)S(1)} collective-permute-done((bf16[256,1536]{1,0:T(8,128)(2,1)S(1)}, bf16[256,1536]{1,0:T(8,128)(2,1)S(1)}, u32[]{:S(2)}, u32[]{:S(2)}) %collective-permute-start) | collective-permute-done | bytes 786464 | tf_op jit(solution)/shard_map/ppermute | solution.py:141
  47.4 1.7 %add_convert_fusion = bf16[256,1536]{1,0:T(8,128)(2,1)} fusion(bf16[256,1536]{1,0:T(8,128)(2,1)S(1)} %collective-permute-done, bf16[256,768]{1,0:T(8,128)(2,1)S(1)} %bitcast.23, bf16[768,1536]{1,0:T(8,128)(2,1)S(1)} %copy-done.3), kind=kOutput, calls=%fused_computation.2 | convolution fusion | flops 605159424 | bytes 4325376 | tf_op jit(solution)/shard_map/dot_general | solution.py:144
  49.0 4.3 %all-to-all-start = ((bf16[4,64,1536]{2,1,0:T(8,128)(2,1)}), bf16[4,64,1536]{2,1,0:T(8,128)(2,1)S(1)}, u32[]{:S(2)}, u32[]{:S(2)}) async-start(bf16[4,64,1536]{2,1,0:T(8,128)(2,1)} %bitcast.22), calls=%async_computation | async-start | bytes 1572864 | tf_op jit(solution)/shard_map/all_to_all | solution.py:147
  53.4 4.4 %collective-permute-start.3 = (bf16[4,2,64,768]{3,2,1,0:T(8,128)(2,1)S(1)}, bf16[4,2,64,768]{3,2,1,0:T(8,128)(2,1)}, u32[]{:S(2)}, u32[]{:S(2)}) collective-permute-start(bf16[4,2,64,768]{3,2,1,0:T(8,128)(2,1)S(1)} %bitcast.19), channel_id=1, source_target_pairs={{0,384},{128,0},{256,128},{384,256},{1,385},{129,1},{257,129},{385... | collective-permute-start | bytes 2359304 | tf_op jit(solution)/shard_map/ppermute | solution.py:150
  57.7 1.9 %collective-permute-start.2 = (bf16[4,2,64,768]{3,2,1,0:T(8,128)(2,1)S(1)}, bf16[4,2,64,768]{3,2,1,0:T(8,128)(2,1)}, u32[]{:S(2)}, u32[]{:S(2)}) collective-permute-start(bf16[4,2,64,768]{3,2,1,0:T(8,128)(2,1)S(1)} %bitcast.20), channel_id=1, source_target_pairs={{0,128},{128,256},{256,384},{384,0},{1,129},{129,257},{257,385},{3... | collective-permute-start | bytes 2359304 | tf_op jit(solution)/shard_map/ppermute | solution.py:149
  59.7 5.4 %all-to-all-done = bf16[4,64,1536]{2,1,0:T(8,128)(2,1)S(1)} async-done(((bf16[4,64,1536]{2,1,0:T(8,128)(2,1)}), bf16[4,64,1536]{2,1,0:T(8,128)(2,1)S(1)}, u32[]{:S(2)}, u32[]{:S(2)}) %all-to-all-start) | async-done | bytes 786464 | tf_op jit(solution)/shard_map/all_to_all | solution.py:147
  65.5 11.7 %all_gather.7.refs_1_ = bf16[256,1536]{1,0:T(8,128)(2,1)S(1)} all-gather(bf16[64,1536]{1,0:T(8,128)(2,1)S(1)} %fusion.2), channel_id=1, replica_groups={{0,32,64,96},{16,48,80,112},{1,33,65,97},{17,49,81,113},{2,34,66,98},{1..., dimensions={0}, use_global_device_ids=true | all-gather | bytes 983040 | tf_op jit(solution)/shard_map/all_gather | solution.py:155
  77.2 5.9 %collective-permute-start.1 = (bf16[256,1536]{1,0:T(8,128)(2,1)S(1)}, bf16[256,1536]{1,0:T(8,128)(2,1)S(1)}, u32[]{:S(2)}, u32[]{:S(2)}) collective-permute-start(bf16[256,1536]{1,0:T(8,128)(2,1)S(1)} %all_gather.7.refs_1_), channel_id=1, source_target_pairs={{0,16},{16,0},{32,48},{48,32},{64,80},{80,64},{96,112},{112,96},{1... | collective-permute-start | bytes 2359304 | tf_op jit(solution)/shard_map/ppermute | solution.py:156
  83.1 4.3 %collective-permute-start.5 = (bf16[256,1536]{1,0:T(8,128)(2,1)S(1)}, bf16[256,1536]{1,0:T(8,128)(2,1)}, u32[]{:S(2)}, u32[]{:S(2)}) collective-permute-start(bf16[256,1536]{1,0:T(8,128)(2,1)S(1)} %all_gather.7.refs_1_), channel_id=1, source_target_pairs={{0,384},{128,0},{256,128},{384,256},{1,385},{129,1},{257,129},{385... | collective-permute-start | bytes 2359304 | tf_op jit(solution)/shard_map/ppermute | solution.py:158
  87.4 1.9 %collective-permute-start.4 = (bf16[256,1536]{1,0:T(8,128)(2,1)S(1)}, bf16[256,1536]{1,0:T(8,128)(2,1)}, u32[]{:S(2)}, u32[]{:S(2)}) collective-permute-start(bf16[256,1536]{1,0:T(8,128)(2,1)S(1)} %all_gather.7.refs_1_), channel_id=1, source_target_pairs={{0,128},{128,256},{256,384},{384,0},{1,129},{129,257},{257,385},{3... | collective-permute-start | bytes 2359304 | tf_op jit(solution)/shard_map/ppermute | solution.py:157
  89.5 1.9 %copy-done.4 = bf16[768,1536]{1,0:T(8,128)(2,1)S(1)} copy-done((bf16[768,1536]{1,0:T(8,128)(2,1)S(1)}, bf16[768,1536]{1,0:T(8,128)(2,1)}, u32[]{:S(2)}) %copy-start.4) | copy-done | bytes 2359320
  91.5 2.7 %tokens_parts.1 = (bf16[128,768]{1,0:T(8,128)(2,1)S(1)}, bf16[128,768]{1,0:T(8,128)(2,1)S(1)}, bf16[128,768]{1,0:T(8,128)(2,1)S(1)}, f32[128,768]{1,0:T(8,128)S(1)}) custom-call(s32[3]{0:T(128)S(1)} %pad_add_fusion.where, bf16[4,64,1536]{2,1,0:T(8,128)(2,1)S(1)} %bitcast.16, bf16[4,64,1536]{2,1,0:T(8,128)(2,1)S(1)} %bitcast.17, bf16[768,1536]{1,0:T(8,128)(2,1)S(1)} %copy-done.4), custom_call_target="tpu_custom_call" | custom-call | flops 1207959552 | bytes 6291456 | tf_op jit(solution)/shard_map/tokens_parts/pallas_call | solution.py:62
  94.1 1.9 %collective-permute-start.6 = (bf16[128,768]{1,0:T(8,128)(2,1)S(1)}, bf16[128,768]{1,0:T(8,128)(2,1)S(1)}, u32[]{:S(2)}, u32[]{:S(2)}) collective-permute-start(bf16[128,768]{1,0:T(8,128)(2,1)S(1)} %get-tuple-element.21), channel_id=1, source_target_pairs={{0,1},{1,2},{2,3},{3,4},{4,5},{5,6},{6,7},{7,8},{8,9},{9,10},{10,1... | collective-permute-start | bytes 589832 | tf_op jit(solution)/shard_map/ppermute | solution.py:168
  96.1 4.6 %collective-permute-start.7 = (bf16[128,768]{1,0:T(8,128)(2,1)S(1)}, bf16[128,768]{1,0:T(8,128)(2,1)S(1)}, u32[]{:S(2)}, u32[]{:S(2)}) collective-permute-start(bf16[128,768]{1,0:T(8,128)(2,1)S(1)} %get-tuple-element.22), channel_id=1, source_target_pairs={{0,15},{1,0},{2,1},{3,2},{4,3},{5,4},{6,5},{7,6},{8,7},{9,8},{10,9... | collective-permute-start | bytes 589832 | tf_op jit(solution)/shard_map/ppermute | solution.py:169
  100.6 3.8 %collective-permute-done.5.refs_7_ = bf16[256,1536]{1,0:T(8,128)(2,1)} collective-permute-done((bf16[256,1536]{1,0:T(8,128)(2,1)S(1)}, bf16[256,1536]{1,0:T(8,128)(2,1)}, u32[]{:S(2)}, u32[]{:S(2)}) %collective-permute-start.5) | collective-permute-done | bytes 786464 | tf_op jit(solution)/shard_map/ppermute | solution.py:158
  104.4 5.1 %collective-permute-done.4.refs_4_ = bf16[256,1536]{1,0:T(8,128)(2,1)} collective-permute-done((bf16[256,1536]{1,0:T(8,128)(2,1)S(1)}, bf16[256,1536]{1,0:T(8,128)(2,1)}, u32[]{:S(2)}, u32[]{:S(2)}) %collective-permute-start.4) | collective-permute-done | bytes 786464 | tf_op jit(solution)/shard_map/ppermute | solution.py:157
  109.5 1.9 %collective-permute-start.12 = (bf16[256,1536]{1,0:T(8,128)(2,1)}, bf16[256,1536]{1,0:T(8,128)(2,1)S(1)}, u32[]{:S(2)}, u32[]{:S(2)}) collective-permute-start(bf16[256,1536]{1,0:T(8,128)(2,1)} %collective-permute-done.5.refs_7_), channel_id=1, source_target_pairs={{0,384},{128,0},{256,128},{384,256},{1,385},{129,1},{257,129},{385... | collective-permute-start | bytes 2359304 | tf_op jit(solution)/shard_map/ppermute | solution.py:173
  111.4 1.9 %collective-permute-start.8 = (bf16[128,768]{1,0:T(8,128)(2,1)S(1)}, bf16[128,768]{1,0:T(8,128)(2,1)S(1)}, u32[]{:S(2)}, u32[]{:S(2)}) collective-permute-start(bf16[128,768]{1,0:T(8,128)(2,1)S(1)} %get-tuple-element.25), channel_id=1, source_target_pairs={{0,2},{1,3},{2,0},{3,1},{4,6},{5,7},{6,4},{7,5},{8,10},{9,11},{10,... | collective-permute-start | bytes 589832 | tf_op jit(solution)/shard_map/ppermute | solution.py:170
  113.4 3.4 %collective-permute-start.11 = (bf16[4,2,64,768]{3,2,1,0:T(8,128)(2,1)}, bf16[4,2,64,768]{3,2,1,0:T(8,128)(2,1)S(1)}, u32[]{:S(2)}, u32[]{:S(2)}) collective-permute-start(bf16[4,2,64,768]{3,2,1,0:T(8,128)(2,1)} %collective-permute-done.2.refs_3_), channel_id=1, source_target_pairs={{0,128},{128,256},{256,384},{384,0},{1,129},{129,257},{257,385},{3... | collective-permute-start | bytes 2359304 | tf_op jit(solution)/shard_map/ppermute | solution.py:174
  116.7 3.8 %collective-permute-start.10 = (bf16[256,1536]{1,0:T(8,128)(2,1)}, bf16[256,1536]{1,0:T(8,128)(2,1)}, u32[]{:S(2)}, u32[]{:S(2)}) collective-permute-start(bf16[256,1536]{1,0:T(8,128)(2,1)} %collective-permute-done.5.refs_7_), channel_id=1, source_target_pairs={{0,16},{16,0},{32,48},{48,32},{64,80},{80,64},{96,112},{112,96},{1... | collective-permute-start | bytes 2359304 | tf_op jit(solution)/shard_map/ppermute | solution.py:176
  120.6 1.9 %collective-permute-start.9 = (bf16[256,1536]{1,0:T(8,128)(2,1)}, bf16[256,1536]{1,0:T(8,128)(2,1)}, u32[]{:S(2)}, u32[]{:S(2)}) collective-permute-start(bf16[256,1536]{1,0:T(8,128)(2,1)} %collective-permute-done.4.refs_4_), channel_id=1, source_target_pairs={{0,16},{16,0},{32,48},{48,32},{64,80},{80,64},{96,112},{112,96},{1... | collective-permute-start | bytes 2359304 | tf_op jit(solution)/shard_map/ppermute | solution.py:175
  122.5 7.0 %collective-permute-done.12.refs_10_ = bf16[256,1536]{1,0:T(8,128)(2,1)S(1)} collective-permute-done((bf16[256,1536]{1,0:T(8,128)(2,1)}, bf16[256,1536]{1,0:T(8,128)(2,1)S(1)}, u32[]{:S(2)}, u32[]{:S(2)}) %collective-permute-start.12) | collective-permute-done | bytes 786464 | tf_op jit(solution)/shard_map/ppermute | solution.py:173
  129.5 3.9 %collective-permute-start.13 = (bf16[256,1536]{1,0:T(8,128)(2,1)S(1)}, bf16[256,1536]{1,0:T(8,128)(2,1)}, u32[]{:S(2)}, u32[]{:S(2)}) collective-permute-start(bf16[256,1536]{1,0:T(8,128)(2,1)S(1)} %collective-permute-done.12.refs_10_), channel_id=1, source_target_pairs={{0,16},{16,0},{32,48},{48,32},{64,80},{80,64},{96,112},{112,96},{1... | collective-permute-start | bytes 2359304 | tf_op jit(solution)/shard_map/ppermute | solution.py:182
  133.5 0.8 add_convert_fusion.1
  134.2 6.2 %all-to-all-start.1 = ((bf16[4,32,768]{2,1,0:T(8,128)(2,1)}), bf16[4,32,768]{2,1,0:T(8,128)(2,1)S(1)}, u32[]{:S(2)}, u32[]{:S(2)}) async-start(bf16[4,32,768]{2,1,0:T(8,128)(2,1)} %bitcast.9), calls=%async_computation.1 | async-start | bytes 393216 | tf_op jit(solution)/shard_map/all_to_all | solution.py:180
  140.5 0.9 copy-done.7
  141.4 9.3 %weight_part.1 = bf16[768,1536]{1,0:T(8,128)(2,1)} custom-call(s32[3]{0:T(128)} %copy-done.2, bf16[4,2,64,768]{3,2,1,0:T(8,128)(2,1)} %bitcast.21, bf16[256,1536]{1,0:T(8,128)(2,1)} %copy-done, bf16[256,1536]{1,0:T(8,128)(2,1)} %copy-done.1, bf16[4,2,64,768]{3,2,1,0:T(8,128)(2,1)} %collective-permute-done.2.refs_3_, ...), custom_call_target="tpu_custom_call" | custom-call | tf_op jit(solution)/shard_map/weight_part/pallas_call | solution.py:107
  150.7 3.6 %all-to-all-done.1 = bf16[4,32,768]{2,1,0:T(8,128)(2,1)S(1)} async-done(((bf16[4,32,768]{2,1,0:T(8,128)(2,1)}), bf16[4,32,768]{2,1,0:T(8,128)(2,1)S(1)}, u32[]{:S(2)}, u32[]{:S(2)}) %all-to-all-start.1) | async-done | bytes 196640 | tf_op jit(solution)/shard_map/all_to_all | solution.py:180
  154.3 0.7 reduce_sum.22
  (30 shorter events, 0.6 us)
Async XLA Ops:
  0.6 34.4 %copy-start.3 = (bf16[768,1536]{1,0:T(8,128)(2,1)S(1)}, bf16[768,1536]{1,0:T(8,128)(2,1)}, u32[]{:S(2)}) copy-start(bf16[768,1536]{1,0:T(8,128)(2,1)} %w.1) | copy-start | bytes 7077892
  35.0 22.8 %copy-start.5 = (bf16[512,768]{1,0:T(8,128)(2,1)}, bf16[512,768]{1,0:T(8,128)(2,1)S(1)}, u32[]{:S(2)}) copy-start(bf16[512,768]{1,0:T(8,128)(2,1)S(1)} %all_gather.6) | copy-start | bytes 2359300
  35.8 11.5 %collective-permute-start = (bf16[256,1536]{1,0:T(8,128)(2,1)S(1)}, bf16[256,1536]{1,0:T(8,128)(2,1)S(1)}, u32[]{:S(2)}, u32[]{:S(2)}) collective-permute-start(bf16[256,1536]{1,0:T(8,128)(2,1)S(1)} %convolution_convert_fusion), channel_id=1, source_target_pairs={{0,16},{16,0},{32,48},{48,32},{64,80},{80,64},{96,112},{112,96},{1... | collective-permute-start | bytes 2359304 | tf_op jit(solution)/shard_map/ppermute | solution.py:141
  49.0 16.1 %copy-start.8 = (bf16[64,1536]{1,0:T(8,128)(2,1)S(1)}, bf16[64,1536]{1,0:T(8,128)(2,1)}, u32[]{:S(2)}) copy-start(bf16[64,1536]{1,0:T(8,128)(2,1)} %param.5) | copy-start | bytes 589828
  49.0 16.0 %all-to-all-start = ((bf16[4,64,1536]{2,1,0:T(8,128)(2,1)}), bf16[4,64,1536]{2,1,0:T(8,128)(2,1)S(1)}, u32[]{:S(2)}, u32[]{:S(2)}) async-start(bf16[4,64,1536]{2,1,0:T(8,128)(2,1)} %bitcast.22), calls=%async_computation | async-start | bytes 1572864 | tf_op jit(solution)/shard_map/all_to_all | solution.py:147
  53.4 36.1 %collective-permute-start.3 = (bf16[4,2,64,768]{3,2,1,0:T(8,128)(2,1)S(1)}, bf16[4,2,64,768]{3,2,1,0:T(8,128)(2,1)}, u32[]{:S(2)}, u32[]{:S(2)}) collective-permute-start(bf16[4,2,64,768]{3,2,1,0:T(8,128)(2,1)S(1)} %bitcast.19), channel_id=1, source_target_pairs={{0,384},{128,0},{256,128},{384,256},{1,385},{129,1},{257,129},{385... | collective-permute-start | bytes 2359304 | tf_op jit(solution)/shard_map/ppermute | solution.py:150
  57.7 31.7 %collective-permute-start.2 = (bf16[4,2,64,768]{3,2,1,0:T(8,128)(2,1)S(1)}, bf16[4,2,64,768]{3,2,1,0:T(8,128)(2,1)}, u32[]{:S(2)}, u32[]{:S(2)}) collective-permute-start(bf16[4,2,64,768]{3,2,1,0:T(8,128)(2,1)S(1)} %bitcast.20), channel_id=1, source_target_pairs={{0,128},{128,256},{256,384},{384,0},{1,129},{129,257},{257,385},{3... | collective-permute-start | bytes 2359304 | tf_op jit(solution)/shard_map/ppermute | solution.py:149
  77.2 57.0 %copy-start = (bf16[256,1536]{1,0:T(8,128)(2,1)}, bf16[256,1536]{1,0:T(8,128)(2,1)S(1)}, u32[]{:S(2)}) copy-start(bf16[256,1536]{1,0:T(8,128)(2,1)S(1)} %all_gather.7.refs_1_) | copy-start | bytes 2359300
  77.2 12.3 %collective-permute-start.1 = (bf16[256,1536]{1,0:T(8,128)(2,1)S(1)}, bf16[256,1536]{1,0:T(8,128)(2,1)S(1)}, u32[]{:S(2)}, u32[]{:S(2)}) collective-permute-start(bf16[256,1536]{1,0:T(8,128)(2,1)S(1)} %all_gather.7.refs_1_), channel_id=1, source_target_pairs={{0,16},{16,0},{32,48},{48,32},{64,80},{80,64},{96,112},{112,96},{1... | collective-permute-start | bytes 2359304 | tf_op jit(solution)/shard_map/ppermute | solution.py:156
  83.1 21.3 %collective-permute-start.5 = (bf16[256,1536]{1,0:T(8,128)(2,1)S(1)}, bf16[256,1536]{1,0:T(8,128)(2,1)}, u32[]{:S(2)}, u32[]{:S(2)}) collective-permute-start(bf16[256,1536]{1,0:T(8,128)(2,1)S(1)} %all_gather.7.refs_1_), channel_id=1, source_target_pairs={{0,384},{128,0},{256,128},{384,256},{1,385},{129,1},{257,129},{385... | collective-permute-start | bytes 2359304 | tf_op jit(solution)/shard_map/ppermute | solution.py:158
  87.4 22.1 %collective-permute-start.4 = (bf16[256,1536]{1,0:T(8,128)(2,1)S(1)}, bf16[256,1536]{1,0:T(8,128)(2,1)}, u32[]{:S(2)}, u32[]{:S(2)}) collective-permute-start(bf16[256,1536]{1,0:T(8,128)(2,1)S(1)} %all_gather.7.refs_1_), channel_id=1, source_target_pairs={{0,128},{128,256},{256,384},{384,0},{1,129},{129,257},{257,385},{3... | collective-permute-start | bytes 2359304 | tf_op jit(solution)/shard_map/ppermute | solution.py:157
  89.5 44.8 %copy-start.2 = (s32[3]{0:T(128)}, s32[3]{0:T(128)S(1)}, u32[]{:S(2)}) copy-start(s32[3]{0:T(128)S(1)} %pad_add_fusion.where) | copy-start | bytes 40
  89.5 44.8 %copy-start.1 = (bf16[256,1536]{1,0:T(8,128)(2,1)}, bf16[256,1536]{1,0:T(8,128)(2,1)S(1)}, u32[]{:S(2)}) copy-start(bf16[256,1536]{1,0:T(8,128)(2,1)S(1)} %collective-permute-done.1.refs_2_) | copy-start | bytes 2359300
  89.5 2.0 %copy-start.4 = (bf16[768,1536]{1,0:T(8,128)(2,1)S(1)}, bf16[768,1536]{1,0:T(8,128)(2,1)}, u32[]{:S(2)}) copy-start(bf16[768,1536]{1,0:T(8,128)(2,1)} %w.1) | copy-start | bytes 7077892
  94.1 15.4 %collective-permute-start.6 = (bf16[128,768]{1,0:T(8,128)(2,1)S(1)}, bf16[128,768]{1,0:T(8,128)(2,1)S(1)}, u32[]{:S(2)}, u32[]{:S(2)}) collective-permute-start(bf16[128,768]{1,0:T(8,128)(2,1)S(1)} %get-tuple-element.21), channel_id=1, source_target_pairs={{0,1},{1,2},{2,3},{3,4},{4,5},{5,6},{6,7},{7,8},{8,9},{9,10},{10,1... | collective-permute-start | bytes 589832 | tf_op jit(solution)/shard_map/ppermute | solution.py:168
  96.1 13.5 %collective-permute-start.7 = (bf16[128,768]{1,0:T(8,128)(2,1)S(1)}, bf16[128,768]{1,0:T(8,128)(2,1)S(1)}, u32[]{:S(2)}, u32[]{:S(2)}) collective-permute-start(bf16[128,768]{1,0:T(8,128)(2,1)S(1)} %get-tuple-element.22), channel_id=1, source_target_pairs={{0,15},{1,0},{2,1},{3,2},{4,3},{5,4},{6,5},{7,6},{8,7},{9,8},{10,9... | collective-permute-start | bytes 589832 | tf_op jit(solution)/shard_map/ppermute | solution.py:169
  109.5 20.0 %collective-permute-start.12 = (bf16[256,1536]{1,0:T(8,128)(2,1)}, bf16[256,1536]{1,0:T(8,128)(2,1)S(1)}, u32[]{:S(2)}, u32[]{:S(2)}) collective-permute-start(bf16[256,1536]{1,0:T(8,128)(2,1)} %collective-permute-done.5.refs_7_), channel_id=1, source_target_pairs={{0,384},{128,0},{256,128},{384,256},{1,385},{129,1},{257,129},{385... | collective-permute-start | bytes 2359304 | tf_op jit(solution)/shard_map/ppermute | solution.py:173
  111.4 22.0 %collective-permute-start.8 = (bf16[128,768]{1,0:T(8,128)(2,1)S(1)}, bf16[128,768]{1,0:T(8,128)(2,1)S(1)}, u32[]{:S(2)}, u32[]{:S(2)}) collective-permute-start(bf16[128,768]{1,0:T(8,128)(2,1)S(1)} %get-tuple-element.25), channel_id=1, source_target_pairs={{0,2},{1,3},{2,0},{3,1},{4,6},{5,7},{6,4},{7,5},{8,10},{9,11},{10,... | collective-permute-start | bytes 589832 | tf_op jit(solution)/shard_map/ppermute | solution.py:170
  113.4 27.1 %collective-permute-start.11 = (bf16[4,2,64,768]{3,2,1,0:T(8,128)(2,1)}, bf16[4,2,64,768]{3,2,1,0:T(8,128)(2,1)S(1)}, u32[]{:S(2)}, u32[]{:S(2)}) collective-permute-start(bf16[4,2,64,768]{3,2,1,0:T(8,128)(2,1)} %collective-permute-done.2.refs_3_), channel_id=1, source_target_pairs={{0,128},{128,256},{256,384},{384,0},{1,129},{129,257},{257,385},{3... | collective-permute-start | bytes 2359304 | tf_op jit(solution)/shard_map/ppermute | solution.py:174
  116.7 23.8 %collective-permute-start.10 = (bf16[256,1536]{1,0:T(8,128)(2,1)}, bf16[256,1536]{1,0:T(8,128)(2,1)}, u32[]{:S(2)}, u32[]{:S(2)}) collective-permute-start(bf16[256,1536]{1,0:T(8,128)(2,1)} %collective-permute-done.5.refs_7_), channel_id=1, source_target_pairs={{0,16},{16,0},{32,48},{48,32},{64,80},{80,64},{96,112},{112,96},{1... | collective-permute-start | bytes 2359304 | tf_op jit(solution)/shard_map/ppermute | solution.py:176
  120.6 19.9 %collective-permute-start.9 = (bf16[256,1536]{1,0:T(8,128)(2,1)}, bf16[256,1536]{1,0:T(8,128)(2,1)}, u32[]{:S(2)}, u32[]{:S(2)}) collective-permute-start(bf16[256,1536]{1,0:T(8,128)(2,1)} %collective-permute-done.4.refs_4_), channel_id=1, source_target_pairs={{0,16},{16,0},{32,48},{48,32},{64,80},{80,64},{96,112},{112,96},{1... | collective-permute-start | bytes 2359304 | tf_op jit(solution)/shard_map/ppermute | solution.py:175
  129.5 11.0 %copy-start.6 = (bf16[256,1536]{1,0:T(8,128)(2,1)}, bf16[256,1536]{1,0:T(8,128)(2,1)S(1)}, u32[]{:S(2)}) copy-start(bf16[256,1536]{1,0:T(8,128)(2,1)S(1)} %collective-permute-done.12.refs_10_) | copy-start | bytes 2359300
  129.5 11.0 %collective-permute-start.13 = (bf16[256,1536]{1,0:T(8,128)(2,1)S(1)}, bf16[256,1536]{1,0:T(8,128)(2,1)}, u32[]{:S(2)}, u32[]{:S(2)}) collective-permute-start(bf16[256,1536]{1,0:T(8,128)(2,1)S(1)} %collective-permute-done.12.refs_10_), channel_id=1, source_target_pairs={{0,16},{16,0},{32,48},{48,32},{64,80},{80,64},{96,112},{112,96},{1... | collective-permute-start | bytes 2359304 | tf_op jit(solution)/shard_map/ppermute | solution.py:182
  134.2 20.0 %all-to-all-start.1 = ((bf16[4,32,768]{2,1,0:T(8,128)(2,1)}), bf16[4,32,768]{2,1,0:T(8,128)(2,1)S(1)}, u32[]{:S(2)}, u32[]{:S(2)}) async-start(bf16[4,32,768]{2,1,0:T(8,128)(2,1)} %bitcast.9), calls=%async_computation.1 | async-start | bytes 393216 | tf_op jit(solution)/shard_map/all_to_all | solution.py:180
  140.5 0.9 copy-start.7

commit v3 on v2

--- a/solution.py
+++ b/solution.py
@@ -9,7 +9,7 @@
 
 F32 = jnp.float32
 BF16 = jnp.bfloat16
-VMEM_LIMIT = 56 * 1024 * 1024
+VMEM_LIMIT = 28 * 1024 * 1024
 TOKENS_VMEM = 24 * 1024 * 1024
 
 
@@ -179,17 +179,12 @@
     col_groups = [[c + 4 * q for q in range(n_col // 4)] for c in range(4)]
     parts = lax.all_to_all(quad, "col", 0, 0, tiled=True, axis_index_groups=col_groups)
 
+    near = weight_part(
+        where, [(panel, own, other), (t_up, up, up_other), (t_down, down, down_other)]
+    )
+    far, near, parts = together((far, near, parts))
     far_other = lax.ppermute(far, "row", other_core)
-    d_weight = weight_part(
-        where,
-        [
-            (panel, own, other),
-            (t_up, up, up_other),
-            (t_down, down, down_other),
-            (t_far, far, far_other),
-        ],
-    )
-    parts, d_weight = together((parts, d_weight))
+    d_weight = weight_part(where, [(t_far, far, far_other)], near)
     d_tokens = parts.reshape(n_col // 4, -1, depth).astype(F32).sum(0).astype(BF16)
     return d_tokens, d_weight
 

time: 156 us -> 151 us (0.968)
  waiting for transfers between devices: 26.8 us -> 15.1 us
  starting transfers between devices: 62 us -> 65.6 us
  local copies, waits for them, and re-layouts: 2.91 us -> 5.69 us
    ppermute x1, waiting for transfers between devices: 7.04 us -> 0.01 us  [per_device(): far = lax.ppermute(down, 'dp', shift(n_dp, -1))]
    unnamed x18, local copies, waits for them, and re-layouts: 2.86 us -> 5.64 us
    ppermute x1, waiting for transfers between devices: 5.11 us -> 2.46 us  [per_device(): up = lax.ppermute(own, 'dp', shift(n_dp, 1))]
    ppermute x1, starting transfers between devices: 1.91 us -> 4.5 us  [per_device(): far = lax.ppermute(down, 'dp', shift(n_dp, -1))]
    ppermute x1, waiting for transfers between devices: 0.01 us -> 2.25 us  [per_device(): t_far = lax.ppermute(t_up, 'dp', shift(n_dp, 1))]
    ppermute x1, starting transfers between devices: 3.93 us -> 6.15 us  [per_device(): far_other = lax.ppermute(far, 'row', other_core)]
    ppermute x1, waiting for transfers between devices: 3.75 us -> 1.63 us  [per_device(): down = lax.ppermute(own, 'dp', shift(n_dp, -1))]
    all_to_all x1, waiting for transfers between devices: 3.58 us -> 1.58 us  [per_device(): lax.all_to_all(quad, 'col', 0, 0, tiled=True, axis_index_groups=col_groups)]
  transfers between devices with their start and end apart: 16 -> 16, of which waited for: 6 -> 6; matrix products, arithmetic and copies ran while one was open for 1% -> 1% of each run, Pallas kernels for 8% -> 6%
where the time goes in v3:
time: 151 us; the launch traced here: 150 us
  starting transfers between devices  65.6 us (43%)
  blocking collectives  45.6 us (30%)
  waiting for transfers between devices  15.1 us (10%)
  Pallas kernels  13.2 us (9%)
  local copies, waits for them, and re-layouts  5.69 us (4%)
  matrix products  2.44 us (2%)
  other arithmetic  1.9 us (1%)
    all_gather x1, blocking collectives, per_device(): panel = lax.all_gather(tokens, 'col', axis=0, tiled=True)  34.3 us
    all_gather x1, blocking collectives, per_device(): lax.all_gather(grad, 'row', axis=0, tiled=True, axis_index_groups=y_groups)  11.3 us
    pallas_call x2, Pallas kernels, weight_part(): pl.pallas_call(functools.partial(weight_kernel, len(terms), len(adds)), g...  10.5 us
    ppermute x1, starting transfers between devices, per_device(): lax.ppermute(jnp.dot(theirs, weight_up, preferred_element_type=F32).astyp...  9.64 us
    ppermute x1, starting transfers between devices, per_device(): other = lax.ppermute(own, 'row', other_core)  6.22 us
    all_to_all x1, starting transfers between devices, per_device(): lax.all_to_all(quad, 'col', 0, 0, tiled=True, axis_index_groups=col_groups)  6.2 us
    ppermute x1, starting transfers between devices, per_device(): far_other = lax.ppermute(far, 'row', other_core)  6.15 us
    unnamed x18, local copies, waits for them, and re-layouts  5.64 us
  transfers between devices with their start and end apart: 16, of which 6 were waited for; matrix products, arithmetic and copies ran while one was open for 1% of the time, Pallas kernels for 6%

profile of v3, /device:TPU:1, one launch (start us, length us, event | category | flops | bytes accessed | tf_op | source)
XLA Modules:
  0.0 150.4 jit_solution(6669920402031590809)
XLA Ops:
  0.7 34.3 %all_gather.6 = bf16[512,768]{1,0:T(8,128)(2,1)S(1)} all-gather(bf16[32,768]{1,0:T(8,128)(2,1)} %param.3), channel_id=1, replica_groups=mesh['dp'=4,'row'=8,'col'=16] {'col'}, dimensions={0}, use_global_device_ids=true | all-gather | bytes 835584 | tf_op jit(solution)/shard_map/all_gather | solution.py:135
  35.8 9.6 %collective-permute-start = (bf16[256,1536]{1,0:T(8,128)(2,1)S(1)}, bf16[256,1536]{1,0:T(8,128)(2,1)S(1)}, u32[]{:S(2)}, u32[]{:S(2)}) collective-permute-start(bf16[256,1536]{1,0:T(8,128)(2,1)S(1)} %convolution_convert_fusion), channel_id=1, source_target_pairs={{0,16},{16,0},{32,48},{48,32},{64,80},{80,64},{96,112},{112,96},{1... | collective-permute-start | bytes 2359304 | tf_op jit(solution)/shard_map/ppermute | solution.py:141
  45.5 1.9 %collective-permute-done = bf16[256,1536]{1,0:T(8,128)(2,1)S(1)} collective-permute-done((bf16[256,1536]{1,0:T(8,128)(2,1)S(1)}, bf16[256,1536]{1,0:T(8,128)(2,1)S(1)}, u32[]{:S(2)}, u32[]{:S(2)}) %collective-permute-start) | collective-permute-done | bytes 786464 | tf_op jit(solution)/shard_map/ppermute | solution.py:141
  47.4 1.7 %add_convert_fusion = bf16[256,1536]{1,0:T(8,128)(2,1)} fusion(bf16[256,1536]{1,0:T(8,128)(2,1)S(1)} %collective-permute-done, bf16[256,768]{1,0:T(8,128)(2,1)S(1)} %bitcast.23, bf16[768,1536]{1,0:T(8,128)(2,1)S(1)} %copy-done.6), kind=kOutput, calls=%fused_computation.2 | convolution fusion | flops 605159424 | bytes 4325376 | tf_op jit(solution)/shard_map/dot_general | solution.py:144
  49.0 4.3 %all-to-all-start = ((bf16[4,64,1536]{2,1,0:T(8,128)(2,1)}), bf16[4,64,1536]{2,1,0:T(8,128)(2,1)S(1)}, u32[]{:S(2)}, u32[]{:S(2)}) async-start(bf16[4,64,1536]{2,1,0:T(8,128)(2,1)} %bitcast.22), calls=%async_computation | async-start | bytes 1572864 | tf_op jit(solution)/shard_map/all_to_all | solution.py:147
  53.4 3.1 %collective-permute-start.4 = (bf16[4,2,64,768]{3,2,1,0:T(8,128)(2,1)S(1)}, bf16[4,2,64,768]{3,2,1,0:T(8,128)(2,1)}, u32[]{:S(2)}, u32[]{:S(2)}) collective-permute-start(bf16[4,2,64,768]{3,2,1,0:T(8,128)(2,1)S(1)} %bitcast.17), channel_id=1, source_target_pairs={{0,128},{128,256},{256,384},{384,0},{1,129},{129,257},{257,385},{3... | collective-permute-start | bytes 2359304 | tf_op jit(solution)/shard_map/ppermute | solution.py:149
  56.5 3.4 %collective-permute-start.5 = (bf16[4,2,64,768]{3,2,1,0:T(8,128)(2,1)S(1)}, bf16[4,2,64,768]{3,2,1,0:T(8,128)(2,1)S(1)}, u32[]{:S(2)}, u32[]{:S(2)}) collective-permute-start(bf16[4,2,64,768]{3,2,1,0:T(8,128)(2,1)S(1)} %bitcast.18), channel_id=1, source_target_pairs={{0,384},{128,0},{256,128},{384,256},{1,385},{129,1},{257,129},{385... | collective-permute-start | bytes 2359304 | tf_op jit(solution)/shard_map/ppermute | solution.py:150
  59.8 5.2 %all-to-all-done = bf16[4,64,1536]{2,1,0:T(8,128)(2,1)S(1)} async-done(((bf16[4,64,1536]{2,1,0:T(8,128)(2,1)}), bf16[4,64,1536]{2,1,0:T(8,128)(2,1)S(1)}, u32[]{:S(2)}, u32[]{:S(2)}) %all-to-all-start) | async-done | bytes 786464 | tf_op jit(solution)/shard_map/all_to_all | solution.py:147
  65.5 11.3 %all_gather.7.refs_1_ = bf16[256,1536]{1,0:T(8,128)(2,1)S(1)} all-gather(bf16[64,1536]{1,0:T(8,128)(2,1)S(1)} %fusion.2), channel_id=1, replica_groups={{0,32,64,96},{16,48,80,112},{1,33,65,97},{17,49,81,113},{2,34,66,98},{1..., dimensions={0}, use_global_device_ids=true | all-gather | bytes 983040 | tf_op jit(solution)/shard_map/all_gather | solution.py:155
  76.8 6.2 %collective-permute-start.3 = (bf16[256,1536]{1,0:T(8,128)(2,1)S(1)}, bf16[256,1536]{1,0:T(8,128)(2,1)S(1)}, u32[]{:S(2)}, u32[]{:S(2)}) collective-permute-start(bf16[256,1536]{1,0:T(8,128)(2,1)S(1)} %all_gather.7.refs_1_), channel_id=1, source_target_pairs={{0,16},{16,0},{32,48},{48,32},{64,80},{80,64},{96,112},{112,96},{1... | collective-permute-start | bytes 2359304 | tf_op jit(solution)/shard_map/ppermute | solution.py:156
  83.1 3.2 %collective-permute-start.1 = (bf16[256,1536]{1,0:T(8,128)(2,1)S(1)}, bf16[256,1536]{1,0:T(8,128)(2,1)}, u32[]{:S(2)}, u32[]{:S(2)}) collective-permute-start(bf16[256,1536]{1,0:T(8,128)(2,1)S(1)} %all_gather.7.refs_1_), channel_id=1, source_target_pairs={{0,128},{128,256},{256,384},{384,0},{1,129},{129,257},{257,385},{3... | collective-permute-start | bytes 2359304 | tf_op jit(solution)/shard_map/ppermute | solution.py:157
  86.3 3.3 %collective-permute-start.2 = (bf16[256,1536]{1,0:T(8,128)(2,1)S(1)}, bf16[256,1536]{1,0:T(8,128)(2,1)}, u32[]{:S(2)}, u32[]{:S(2)}) collective-permute-start(bf16[256,1536]{1,0:T(8,128)(2,1)S(1)} %all_gather.7.refs_1_), channel_id=1, source_target_pairs={{0,384},{128,0},{256,128},{384,256},{1,385},{129,1},{257,129},{385... | collective-permute-start | bytes 2359304 | tf_op jit(solution)/shard_map/ppermute | solution.py:158
  89.7 2.2 %copy-done.7 = bf16[768,1536]{1,0:T(8,128)(2,1)S(1)} copy-done((bf16[768,1536]{1,0:T(8,128)(2,1)S(1)}, bf16[768,1536]{1,0:T(8,128)(2,1)}, u32[]{:S(2)}) %copy-start.7) | copy-done | bytes 2359320
  92.0 2.6 %tokens_parts.1 = (bf16[128,768]{1,0:T(8,128)(2,1)S(1)}, bf16[128,768]{1,0:T(8,128)(2,1)S(1)}, bf16[128,768]{1,0:T(8,128)(2,1)S(1)}, f32[128,768]{1,0:T(8,128)S(1)}) custom-call(s32[3]{0:T(128)S(1)} %pad_add_fusion.where, bf16[4,64,1536]{2,1,0:T(8,128)(2,1)S(1)} %bitcast.20, bf16[4,64,1536]{2,1,0:T(8,128)(2,1)S(1)} %bitcast.21, bf16[768,1536]{1,0:T(8,128)(2,1)S(1)} %copy-done.7), custom_call_target="tpu_custom_call" | custom-call | flops 1207959552 | bytes 6291456 | tf_op jit(solution)/shard_map/tokens_parts/pallas_call | solution.py:62
  94.6 1.9 %collective-permute-start.6 = (bf16[128,768]{1,0:T(8,128)(2,1)S(1)}, bf16[128,768]{1,0:T(8,128)(2,1)S(1)}, u32[]{:S(2)}, u32[]{:S(2)}) collective-permute-start(bf16[128,768]{1,0:T(8,128)(2,1)S(1)} %get-tuple-element.21), channel_id=1, source_target_pairs={{0,1},{1,2},{2,3},{3,4},{4,5},{5,6},{6,7},{7,8},{8,9},{9,10},{10,1... | collective-permute-start | bytes 589832 | tf_op jit(solution)/shard_map/ppermute | solution.py:168
  96.5 4.6 %collective-permute-start.7 = (bf16[128,768]{1,0:T(8,128)(2,1)S(1)}, bf16[128,768]{1,0:T(8,128)(2,1)S(1)}, u32[]{:S(2)}, u32[]{:S(2)}) collective-permute-start(bf16[128,768]{1,0:T(8,128)(2,1)S(1)} %get-tuple-element.22), channel_id=1, source_target_pairs={{0,15},{1,0},{2,1},{3,2},{4,3},{5,4},{6,5},{7,6},{8,7},{9,8},{10,9... | collective-permute-start | bytes 589832 | tf_op jit(solution)/shard_map/ppermute | solution.py:169
  101.1 1.9 %collective-permute-start.11 = (bf16[128,768]{1,0:T(8,128)(2,1)S(1)}, bf16[128,768]{1,0:T(8,128)(2,1)S(1)}, u32[]{:S(2)}, u32[]{:S(2)}) collective-permute-start(bf16[128,768]{1,0:T(8,128)(2,1)S(1)} %get-tuple-element.30), channel_id=1, source_target_pairs={{0,2},{1,3},{2,0},{3,1},{4,6},{5,7},{6,4},{7,5},{8,10},{9,11},{10,... | collective-permute-start | bytes 589832 | tf_op jit(solution)/shard_map/ppermute | solution.py:170
  103.0 2.5 %collective-permute-done.1.refs_4_ = bf16[256,1536]{1,0:T(8,128)(2,1)} collective-permute-done((bf16[256,1536]{1,0:T(8,128)(2,1)S(1)}, bf16[256,1536]{1,0:T(8,128)(2,1)}, u32[]{:S(2)}, u32[]{:S(2)}) %collective-permute-start.1) | collective-permute-done | bytes 786464 | tf_op jit(solution)/shard_map/ppermute | solution.py:157
  105.5 1.6 %collective-permute-done.2.refs_7_ = bf16[256,1536]{1,0:T(8,128)(2,1)} collective-permute-done((bf16[256,1536]{1,0:T(8,128)(2,1)S(1)}, bf16[256,1536]{1,0:T(8,128)(2,1)}, u32[]{:S(2)}, u32[]{:S(2)}) %collective-permute-start.2) | collective-permute-done | bytes 786464 | tf_op jit(solution)/shard_map/ppermute | solution.py:158
  107.2 3.0 %collective-permute-start.10 = (bf16[256,1536]{1,0:T(8,128)(2,1)}, bf16[256,1536]{1,0:T(8,128)(2,1)}, u32[]{:S(2)}, u32[]{:S(2)}) collective-permute-start(bf16[256,1536]{1,0:T(8,128)(2,1)} %collective-permute-done.2.refs_7_), channel_id=1, source_target_pairs={{0,16},{16,0},{32,48},{48,32},{64,80},{80,64},{96,112},{112,96},{1... | collective-permute-start | bytes 2359304 | tf_op jit(solution)/shard_map/ppermute | solution.py:176
  110.2 4.5 %collective-permute-start.8 = (bf16[256,1536]{1,0:T(8,128)(2,1)}, bf16[256,1536]{1,0:T(8,128)(2,1)}, u32[]{:S(2)}, u32[]{:S(2)}) collective-permute-start(bf16[256,1536]{1,0:T(8,128)(2,1)} %collective-permute-done.2.refs_7_), channel_id=1, source_target_pairs={{0,384},{128,0},{256,128},{384,256},{1,385},{129,1},{257,129},{385... | collective-permute-start | bytes 2359304 | tf_op jit(solution)/shard_map/ppermute | solution.py:173
  114.7 2.2 %collective-permute-start.9 = (bf16[256,1536]{1,0:T(8,128)(2,1)}, bf16[256,1536]{1,0:T(8,128)(2,1)}, u32[]{:S(2)}, u32[]{:S(2)}) collective-permute-start(bf16[256,1536]{1,0:T(8,128)(2,1)} %collective-permute-done.1.refs_4_), channel_id=1, source_target_pairs={{0,16},{16,0},{32,48},{48,32},{64,80},{80,64},{96,112},{112,96},{1... | collective-permute-start | bytes 2359304 | tf_op jit(solution)/shard_map/ppermute | solution.py:175
  117.7 6.2 %all-to-all-start.1 = ((bf16[4,32,768]{2,1,0:T(8,128)(2,1)}), bf16[4,32,768]{2,1,0:T(8,128)(2,1)S(1)}, u32[]{:S(2)}, u32[]{:S(2)}) async-start(bf16[4,32,768]{2,1,0:T(8,128)(2,1)} %bitcast.9), calls=%async_computation.1 | async-start | bytes 393216 | tf_op jit(solution)/shard_map/all_to_all | solution.py:180
  123.9 1.9 %collective-permute-start.12 = (bf16[4,2,64,768]{3,2,1,0:T(8,128)(2,1)}, bf16[4,2,64,768]{3,2,1,0:T(8,128)(2,1)}, u32[]{:S(2)}, u32[]{:S(2)}) collective-permute-start(bf16[4,2,64,768]{3,2,1,0:T(8,128)(2,1)} %collective-permute-done.4.refs_3_), channel_id=1, source_target_pairs={{0,128},{128,256},{256,384},{384,0},{1,129},{129,257},{257,385},{3... | collective-permute-start | bytes 2359304 | tf_op jit(solution)/shard_map/ppermute | solution.py:174
  125.8 1.1 copy-done.1
  127.0 1.1 copy-done.3
  128.1 1.1 copy-done.5
  129.2 6.0 %weight_part.2.refs_3_ = bf16[768,1536]{1,0:T(8,128)(2,1)S(1)} custom-call(s32[3]{0:T(128)S(1)} %pad_add_fusion.where, bf16[4,2,64,768]{3,2,1,0:T(8,128)(2,1)S(1)} %bitcast.19, bf16[256,1536]{1,0:T(8,128)(2,1)S(1)} %copy-done.1, bf16[256,1536]{1,0:T(8,128)(2,1)S(1)} %copy-done.5, bf16[4,2,64,768]{3,2,1,0:T(8,128)(2,1)} %collective-permute-done.4.refs_3_, ...), custom_call_target="tpu_custom_call" | custom-call | tf_op jit(solution)/shard_map/weight_part/pallas_call | solution.py:107
  135.3 1.6 %all-to-all-done.1 = bf16[4,32,768]{2,1,0:T(8,128)(2,1)S(1)} async-done(((bf16[4,32,768]{2,1,0:T(8,128)(2,1)}), bf16[4,32,768]{2,1,0:T(8,128)(2,1)S(1)}, u32[]{:S(2)}, u32[]{:S(2)}) %all-to-all-start.1) | async-done | bytes 196640 | tf_op jit(solution)/shard_map/all_to_all | solution.py:180
  136.8 6.1 %collective-permute-start.13 = (bf16[256,1536]{1,0:T(8,128)(2,1)}, bf16[256,1536]{1,0:T(8,128)(2,1)S(1)}, u32[]{:S(2)}, u32[]{:S(2)}) collective-permute-start(bf16[256,1536]{1,0:T(8,128)(2,1)} %collective-permute-done.8.refs_1_), channel_id=1, source_target_pairs={{0,16},{16,0},{32,48},{48,32},{64,80},{80,64},{96,112},{112,96},{1... | collective-permute-start | bytes 2359304 | tf_op jit(solution)/shard_map/ppermute | solution.py:186
  143.6 2.2 %collective-permute-done.12.refs_0_ = bf16[4,2,64,768]{3,2,1,0:T(8,128)(2,1)} collective-permute-done((bf16[4,2,64,768]{3,2,1,0:T(8,128)(2,1)}, bf16[4,2,64,768]{3,2,1,0:T(8,128)(2,1)}, u32[]{:S(2)}, u32[]{:S(2)}) %collective-permute-start.12) | collective-permute-done | bytes 786464 | tf_op jit(solution)/shard_map/ppermute | solution.py:174
  145.9 4.5 %weight_part.3 = bf16[768,1536]{1,0:T(8,128)(2,1)} custom-call(s32[3]{0:T(128)S(1)} %pad_add_fusion.where, bf16[4,2,64,768]{3,2,1,0:T(8,128)(2,1)} %collective-permute-done.12.refs_0_, bf16[256,1536]{1,0:T(8,128)(2,1)} %collective-permute-done.8.refs_1_, bf16[256,1536]{1,0:T(8,128)(2,1)S(1)} %collective-permute-done.13.refs_2_, ...), custom_call_target="tpu_custom_call" | custom-call | tf_op jit(solution)/shard_map/weight_part/pallas_call | solution.py:107
  (31 shorter events, 2.8 us)
Async XLA Ops:
  0.6 34.4 %copy-start.6 = (bf16[768,1536]{1,0:T(8,128)(2,1)S(1)}, bf16[768,1536]{1,0:T(8,128)(2,1)}, u32[]{:S(2)}) copy-start(bf16[768,1536]{1,0:T(8,128)(2,1)} %w.1) | copy-start | bytes 7077892
  35.8 11.5 %collective-permute-start = (bf16[256,1536]{1,0:T(8,128)(2,1)S(1)}, bf16[256,1536]{1,0:T(8,128)(2,1)S(1)}, u32[]{:S(2)}, u32[]{:S(2)}) collective-permute-start(bf16[256,1536]{1,0:T(8,128)(2,1)S(1)} %convolution_convert_fusion), channel_id=1, source_target_pairs={{0,16},{16,0},{32,48},{48,32},{64,80},{80,64},{96,112},{112,96},{1... | collective-permute-start | bytes 2359304 | tf_op jit(solution)/shard_map/ppermute | solution.py:141
  49.0 16.2 %copy-start.8 = (bf16[64,1536]{1,0:T(8,128)(2,1)S(1)}, bf16[64,1536]{1,0:T(8,128)(2,1)}, u32[]{:S(2)}) copy-start(bf16[64,1536]{1,0:T(8,128)(2,1)} %param.5) | copy-start | bytes 589828
  49.0 16.0 %all-to-all-start = ((bf16[4,64,1536]{2,1,0:T(8,128)(2,1)}), bf16[4,64,1536]{2,1,0:T(8,128)(2,1)S(1)}, u32[]{:S(2)}, u32[]{:S(2)}) async-start(bf16[4,64,1536]{2,1,0:T(8,128)(2,1)} %bitcast.22), calls=%async_computation | async-start | bytes 1572864 | tf_op jit(solution)/shard_map/all_to_all | solution.py:147
  53.4 36.3 %collective-permute-start.4 = (bf16[4,2,64,768]{3,2,1,0:T(8,128)(2,1)S(1)}, bf16[4,2,64,768]{3,2,1,0:T(8,128)(2,1)}, u32[]{:S(2)}, u32[]{:S(2)}) collective-permute-start(bf16[4,2,64,768]{3,2,1,0:T(8,128)(2,1)S(1)} %bitcast.17), channel_id=1, source_target_pairs={{0,128},{128,256},{256,384},{384,0},{1,129},{129,257},{257,385},{3... | collective-permute-start | bytes 2359304 | tf_op jit(solution)/shard_map/ppermute | solution.py:149
  56.5 33.2 %collective-permute-start.5 = (bf16[4,2,64,768]{3,2,1,0:T(8,128)(2,1)S(1)}, bf16[4,2,64,768]{3,2,1,0:T(8,128)(2,1)S(1)}, u32[]{:S(2)}, u32[]{:S(2)}) collective-permute-start(bf16[4,2,64,768]{3,2,1,0:T(8,128)(2,1)S(1)} %bitcast.18), channel_id=1, source_target_pairs={{0,384},{128,0},{256,128},{384,256},{1,385},{129,1},{257,129},{385... | collective-permute-start | bytes 2359304 | tf_op jit(solution)/shard_map/ppermute | solution.py:150
  76.8 40.9 %copy-start = (bf16[256,1536]{1,0:T(8,128)(2,1)}, bf16[256,1536]{1,0:T(8,128)(2,1)S(1)}, u32[]{:S(2)}) copy-start(bf16[256,1536]{1,0:T(8,128)(2,1)S(1)} %all_gather.7.refs_1_) | copy-start | bytes 2359300
  76.8 12.9 %collective-permute-start.3 = (bf16[256,1536]{1,0:T(8,128)(2,1)S(1)}, bf16[256,1536]{1,0:T(8,128)(2,1)S(1)}, u32[]{:S(2)}, u32[]{:S(2)}) collective-permute-start(bf16[256,1536]{1,0:T(8,128)(2,1)S(1)} %all_gather.7.refs_1_), channel_id=1, source_target_pairs={{0,16},{16,0},{32,48},{48,32},{64,80},{80,64},{96,112},{112,96},{1... | collective-permute-start | bytes 2359304 | tf_op jit(solution)/shard_map/ppermute | solution.py:156
  83.1 22.5 %collective-permute-start.1 = (bf16[256,1536]{1,0:T(8,128)(2,1)S(1)}, bf16[256,1536]{1,0:T(8,128)(2,1)}, u32[]{:S(2)}, u32[]{:S(2)}) collective-permute-start(bf16[256,1536]{1,0:T(8,128)(2,1)S(1)} %all_gather.7.refs_1_), channel_id=1, source_target_pairs={{0,128},{128,256},{256,384},{384,0},{1,129},{129,257},{257,385},{3... | collective-permute-start | bytes 2359304 | tf_op jit(solution)/shard_map/ppermute | solution.py:157
  86.3 20.8 %collective-permute-start.2 = (bf16[256,1536]{1,0:T(8,128)(2,1)S(1)}, bf16[256,1536]{1,0:T(8,128)(2,1)}, u32[]{:S(2)}, u32[]{:S(2)}) collective-permute-start(bf16[256,1536]{1,0:T(8,128)(2,1)S(1)} %all_gather.7.refs_1_), channel_id=1, source_target_pairs={{0,384},{128,0},{256,128},{384,256},{1,385},{129,1},{257,129},{385... | collective-permute-start | bytes 2359304 | tf_op jit(solution)/shard_map/ppermute | solution.py:158
  89.7 28.0 %copy-start.2 = (bf16[4,2,64,768]{3,2,1,0:T(8,128)(2,1)}, bf16[4,2,64,768]{3,2,1,0:T(8,128)(2,1)S(1)}, u32[]{:S(2)}) copy-start(bf16[4,2,64,768]{3,2,1,0:T(8,128)(2,1)S(1)} %collective-permute-done.5.refs_6_) | copy-start | bytes 2359300
  89.7 28.0 %copy-start.4 = (bf16[256,1536]{1,0:T(8,128)(2,1)}, bf16[256,1536]{1,0:T(8,128)(2,1)S(1)}, u32[]{:S(2)}) copy-start(bf16[256,1536]{1,0:T(8,128)(2,1)S(1)} %collective-permute-done.3.refs_2_) | copy-start | bytes 2359300
  89.7 2.2 %copy-start.7 = (bf16[768,1536]{1,0:T(8,128)(2,1)S(1)}, bf16[768,1536]{1,0:T(8,128)(2,1)}, u32[]{:S(2)}) copy-start(bf16[768,1536]{1,0:T(8,128)(2,1)} %w.1) | copy-start | bytes 7077892
  94.6 12.5 %collective-permute-start.6 = (bf16[128,768]{1,0:T(8,128)(2,1)S(1)}, bf16[128,768]{1,0:T(8,128)(2,1)S(1)}, u32[]{:S(2)}, u32[]{:S(2)}) collective-permute-start(bf16[128,768]{1,0:T(8,128)(2,1)S(1)} %get-tuple-element.21), channel_id=1, source_target_pairs={{0,1},{1,2},{2,3},{3,4},{4,5},{5,6},{6,7},{7,8},{8,9},{9,10},{10,1... | collective-permute-start | bytes 589832 | tf_op jit(solution)/shard_map/ppermute | solution.py:168
  96.5 10.6 %collective-permute-start.7 = (bf16[128,768]{1,0:T(8,128)(2,1)S(1)}, bf16[128,768]{1,0:T(8,128)(2,1)S(1)}, u32[]{:S(2)}, u32[]{:S(2)}) collective-permute-start(bf16[128,768]{1,0:T(8,128)(2,1)S(1)} %get-tuple-element.22), channel_id=1, source_target_pairs={{0,15},{1,0},{2,1},{3,2},{4,3},{5,4},{6,5},{7,6},{8,7},{9,8},{10,9... | collective-permute-start | bytes 589832 | tf_op jit(solution)/shard_map/ppermute | solution.py:169
  101.1 15.8 %collective-permute-start.11 = (bf16[128,768]{1,0:T(8,128)(2,1)S(1)}, bf16[128,768]{1,0:T(8,128)(2,1)S(1)}, u32[]{:S(2)}, u32[]{:S(2)}) collective-permute-start(bf16[128,768]{1,0:T(8,128)(2,1)S(1)} %get-tuple-element.30), channel_id=1, source_target_pairs={{0,2},{1,3},{2,0},{3,1},{4,6},{5,7},{6,4},{7,5},{8,10},{9,11},{10,... | collective-permute-start | bytes 589832 | tf_op jit(solution)/shard_map/ppermute | solution.py:170
  107.2 18.7 %collective-permute-start.10 = (bf16[256,1536]{1,0:T(8,128)(2,1)}, bf16[256,1536]{1,0:T(8,128)(2,1)}, u32[]{:S(2)}, u32[]{:S(2)}) collective-permute-start(bf16[256,1536]{1,0:T(8,128)(2,1)} %collective-permute-done.2.refs_7_), channel_id=1, source_target_pairs={{0,16},{16,0},{32,48},{48,32},{64,80},{80,64},{96,112},{112,96},{1... | collective-permute-start | bytes 2359304 | tf_op jit(solution)/shard_map/ppermute | solution.py:176
  110.2 26.7 %collective-permute-start.8 = (bf16[256,1536]{1,0:T(8,128)(2,1)}, bf16[256,1536]{1,0:T(8,128)(2,1)}, u32[]{:S(2)}, u32[]{:S(2)}) collective-permute-start(bf16[256,1536]{1,0:T(8,128)(2,1)} %collective-permute-done.2.refs_7_), channel_id=1, source_target_pairs={{0,384},{128,0},{256,128},{384,256},{1,385},{129,1},{257,129},{385... | collective-permute-start | bytes 2359304 | tf_op jit(solution)/shard_map/ppermute | solution.py:173
  114.7 11.1 %collective-permute-start.9 = (bf16[256,1536]{1,0:T(8,128)(2,1)}, bf16[256,1536]{1,0:T(8,128)(2,1)}, u32[]{:S(2)}, u32[]{:S(2)}) collective-permute-start(bf16[256,1536]{1,0:T(8,128)(2,1)} %collective-permute-done.1.refs_4_), channel_id=1, source_target_pairs={{0,16},{16,0},{32,48},{48,32},{64,80},{80,64},{96,112},{112,96},{1... | collective-permute-start | bytes 2359304 | tf_op jit(solution)/shard_map/ppermute | solution.py:175
  117.7 19.2 %all-to-all-start.1 = ((bf16[4,32,768]{2,1,0:T(8,128)(2,1)}), bf16[4,32,768]{2,1,0:T(8,128)(2,1)S(1)}, u32[]{:S(2)}, u32[]{:S(2)}) async-start(bf16[4,32,768]{2,1,0:T(8,128)(2,1)} %bitcast.9), calls=%async_computation.1 | async-start | bytes 393216 | tf_op jit(solution)/shard_map/all_to_all | solution.py:180
  123.9 22.0 %collective-permute-start.12 = (bf16[4,2,64,768]{3,2,1,0:T(8,128)(2,1)}, bf16[4,2,64,768]{3,2,1,0:T(8,128)(2,1)}, u32[]{:S(2)}, u32[]{:S(2)}) collective-permute-start(bf16[4,2,64,768]{3,2,1,0:T(8,128)(2,1)} %collective-permute-done.4.refs_3_), channel_id=1, source_target_pairs={{0,128},{128,256},{256,384},{384,0},{1,129},{129,257},{257,385},{3... | collective-permute-start | bytes 2359304 | tf_op jit(solution)/shard_map/ppermute | solution.py:174
  125.8 1.1 copy-start.1
  127.0 1.1 copy-start.3
  128.1 1.1 copy-start.5
  136.8 9.1 %collective-permute-start.13 = (bf16[256,1536]{1,0:T(8,128)(2,1)}, bf16[256,1536]{1,0:T(8,128)(2,1)S(1)}, u32[]{:S(2)}, u32[]{:S(2)}) collective-permute-start(bf16[256,1536]{1,0:T(8,128)(2,1)} %collective-permute-done.8.refs_1_), channel_id=1, source_target_pairs={{0,16},{16,0},{32,48},{48,32},{64,80},{80,64},{96,112},{112,96},{1... | collective-permute-start | bytes 2359304 | tf_op jit(solution)/shard_map/ppermute | solution.py:186

commit v4 on v3

--- a/solution.py
+++ b/solution.py
@@ -182,7 +182,7 @@
     near = weight_part(
         where, [(panel, own, other), (t_up, up, up_other), (t_down, down, down_other)]
     )
-    far, near, parts = together((far, near, parts))
+    far, near, parts, t_far = together((far, near, parts, t_far))
     far_other = lax.ppermute(far, "row", other_core)
     d_weight = weight_part(where, [(t_far, far, far_other)], near)
     d_tokens = parts.reshape(n_col // 4, -1, depth).astype(F32).sum(0).astype(BF16)

time: 151 us -> 151 us (level)
    ppermute x1, waiting for transfers between devices: 2.25 us -> 0.01 us  [per_device(): t_far = lax.ppermute(t_up, 'dp', shift(n_dp, 1))]
    all_to_all x1, waiting for transfers between devices: 1.58 us -> 3.5 us  [per_device(): lax.all_to_all(quad, 'col', 0, 0, tiled=True, axis_index_groups=col_groups)]
    ppermute x1, waiting for transfers between devices: 1.63 us -> 0.01 us  [per_device(): down = lax.ppermute(own, 'dp', shift(n_dp, -1))]
  transfers between devices with their start and end apart: 16 -> 16, of which waited for: 6 -> 5; matrix products, arithmetic and copies ran while one was open for 1% -> 1% of each run, Pallas kernels for 6% -> 6%
where the time goes in v4:
time: 151 us; the launch traced here: 150 us
  starting transfers between devices  65.5 us (43%)
  blocking collectives  45.6 us (30%)
  waiting for transfers between devices  14.5 us (10%)
  Pallas kernels  13.2 us (9%)
  local copies, waits for them, and re-layouts  5.69 us (4%)
  matrix products  2.44 us (2%)
  other arithmetic  1.9 us (1%)
    all_gather x1, blocking collectives, per_device(): panel = lax.all_gather(tokens, 'col', axis=0, tiled=True)  34.3 us
    all_gather x1, blocking collectives, per_device(): lax.all_gather(grad, 'row', axis=0, tiled=True, axis_index_groups=y_groups)  11.3 us
    pallas_call x2, Pallas kernels, weight_part(): pl.pallas_call(functools.partial(weight_kernel, len(terms), len(adds)), g...  10.5 us
    ppermute x1, starting transfers between devices, per_device(): lax.ppermute(jnp.dot(theirs, weight_up, preferred_element_type=F32).astyp...  9.64 us
    ppermute x1, starting transfers between devices, per_device(): other = lax.ppermute(own, 'row', other_core)  6.22 us
    all_to_all x1, starting transfers between devices, per_device(): lax.all_to_all(quad, 'col', 0, 0, tiled=True, axis_index_groups=col_groups)  6.2 us
    ppermute x1, starting transfers between devices, per_device(): far_other = lax.ppermute(far, 'row', other_core)  6.1 us
    unnamed x18, local copies, waits for them, and re-layouts  5.64 us
  transfers between devices with their start and end apart: 16, of which 5 were waited for; matrix products, arithmetic and copies ran while one was open for 1% of the time, Pallas kernels for 6%

profile of v4, /device:TPU:1, one launch (start us, length us, event | category | flops | bytes accessed | tf_op | source)
XLA Modules:
  0.0 149.9 jit_solution(5196284003498444039)
XLA Ops:
  0.7 34.3 %all_gather.6 = bf16[512,768]{1,0:T(8,128)(2,1)S(1)} all-gather(bf16[32,768]{1,0:T(8,128)(2,1)} %param.3), channel_id=1, replica_groups=mesh['dp'=4,'row'=8,'col'=16] {'col'}, dimensions={0}, use_global_device_ids=true | all-gather | bytes 835584 | tf_op jit(solution)/shard_map/all_gather | solution.py:135
  35.8 9.6 %collective-permute-start = (bf16[256,1536]{1,0:T(8,128)(2,1)S(1)}, bf16[256,1536]{1,0:T(8,128)(2,1)S(1)}, u32[]{:S(2)}, u32[]{:S(2)}) collective-permute-start(bf16[256,1536]{1,0:T(8,128)(2,1)S(1)} %convolution_convert_fusion), channel_id=1, source_target_pairs={{0,16},{16,0},{32,48},{48,32},{64,80},{80,64},{96,112},{112,96},{1... | collective-permute-start | bytes 2359304 | tf_op jit(solution)/shard_map/ppermute | solution.py:141
  45.5 1.9 %collective-permute-done = bf16[256,1536]{1,0:T(8,128)(2,1)S(1)} collective-permute-done((bf16[256,1536]{1,0:T(8,128)(2,1)S(1)}, bf16[256,1536]{1,0:T(8,128)(2,1)S(1)}, u32[]{:S(2)}, u32[]{:S(2)}) %collective-permute-start) | collective-permute-done | bytes 786464 | tf_op jit(solution)/shard_map/ppermute | solution.py:141
  47.4 1.7 %add_convert_fusion = bf16[256,1536]{1,0:T(8,128)(2,1)} fusion(bf16[256,1536]{1,0:T(8,128)(2,1)S(1)} %collective-permute-done, bf16[256,768]{1,0:T(8,128)(2,1)S(1)} %bitcast.23, bf16[768,1536]{1,0:T(8,128)(2,1)S(1)} %copy-done.6), kind=kOutput, calls=%fused_computation.2 | convolution fusion | flops 605159424 | bytes 4325376 | tf_op jit(solution)/shard_map/dot_general | solution.py:144
  49.0 4.3 %all-to-all-start = ((bf16[4,64,1536]{2,1,0:T(8,128)(2,1)}), bf16[4,64,1536]{2,1,0:T(8,128)(2,1)S(1)}, u32[]{:S(2)}, u32[]{:S(2)}) async-start(bf16[4,64,1536]{2,1,0:T(8,128)(2,1)} %bitcast.22), calls=%async_computation | async-start | bytes 1572864 | tf_op jit(solution)/shard_map/all_to_all | solution.py:147
  53.4 3.1 %collective-permute-start.4 = (bf16[4,2,64,768]{3,2,1,0:T(8,128)(2,1)S(1)}, bf16[4,2,64,768]{3,2,1,0:T(8,128)(2,1)}, u32[]{:S(2)}, u32[]{:S(2)}) collective-permute-start(bf16[4,2,64,768]{3,2,1,0:T(8,128)(2,1)S(1)} %bitcast.17), channel_id=1, source_target_pairs={{0,128},{128,256},{256,384},{384,0},{1,129},{129,257},{257,385},{3... | collective-permute-start | bytes 2359304 | tf_op jit(solution)/shard_map/ppermute | solution.py:149
  56.5 3.4 %collective-permute-start.5 = (bf16[4,2,64,768]{3,2,1,0:T(8,128)(2,1)S(1)}, bf16[4,2,64,768]{3,2,1,0:T(8,128)(2,1)S(1)}, u32[]{:S(2)}, u32[]{:S(2)}) collective-permute-start(bf16[4,2,64,768]{3,2,1,0:T(8,128)(2,1)S(1)} %bitcast.18), channel_id=1, source_target_pairs={{0,384},{128,0},{256,128},{384,256},{1,385},{129,1},{257,129},{385... | collective-permute-start | bytes 2359304 | tf_op jit(solution)/shard_map/ppermute | solution.py:150
  59.8 5.2 %all-to-all-done = bf16[4,64,1536]{2,1,0:T(8,128)(2,1)S(1)} async-done(((bf16[4,64,1536]{2,1,0:T(8,128)(2,1)}), bf16[4,64,1536]{2,1,0:T(8,128)(2,1)S(1)}, u32[]{:S(2)}, u32[]{:S(2)}) %all-to-all-start) | async-done | bytes 786464 | tf_op jit(solution)/shard_map/all_to_all | solution.py:147
  65.5 11.3 %all_gather.7.refs_1_ = bf16[256,1536]{1,0:T(8,128)(2,1)S(1)} all-gather(bf16[64,1536]{1,0:T(8,128)(2,1)S(1)} %fusion.2), channel_id=1, replica_groups={{0,32,64,96},{16,48,80,112},{1,33,65,97},{17,49,81,113},{2,34,66,98},{1..., dimensions={0}, use_global_device_ids=true | all-gather | bytes 983040 | tf_op jit(solution)/shard_map/all_gather | solution.py:155
  76.8 6.2 %collective-permute-start.3 = (bf16[256,1536]{1,0:T(8,128)(2,1)S(1)}, bf16[256,1536]{1,0:T(8,128)(2,1)S(1)}, u32[]{:S(2)}, u32[]{:S(2)}) collective-permute-start(bf16[256,1536]{1,0:T(8,128)(2,1)S(1)} %all_gather.7.refs_1_), channel_id=1, source_target_pairs={{0,16},{16,0},{32,48},{48,32},{64,80},{80,64},{96,112},{112,96},{1... | collective-permute-start | bytes 2359304 | tf_op jit(solution)/shard_map/ppermute | solution.py:156
  83.1 3.2 %collective-permute-start.1 = (bf16[256,1536]{1,0:T(8,128)(2,1)S(1)}, bf16[256,1536]{1,0:T(8,128)(2,1)}, u32[]{:S(2)}, u32[]{:S(2)}) collective-permute-start(bf16[256,1536]{1,0:T(8,128)(2,1)S(1)} %all_gather.7.refs_1_), channel_id=1, source_target_pairs={{0,128},{128,256},{256,384},{384,0},{1,129},{129,257},{257,385},{3... | collective-permute-start | bytes 2359304 | tf_op jit(solution)/shard_map/ppermute | solution.py:157
  86.3 3.3 %collective-permute-start.2 = (bf16[256,1536]{1,0:T(8,128)(2,1)S(1)}, bf16[256,1536]{1,0:T(8,128)(2,1)}, u32[]{:S(2)}, u32[]{:S(2)}) collective-permute-start(bf16[256,1536]{1,0:T(8,128)(2,1)S(1)} %all_gather.7.refs_1_), channel_id=1, source_target_pairs={{0,384},{128,0},{256,128},{384,256},{1,385},{129,1},{257,129},{385... | collective-permute-start | bytes 2359304 | tf_op jit(solution)/shard_map/ppermute | solution.py:158
  89.7 2.2 %copy-done.7 = bf16[768,1536]{1,0:T(8,128)(2,1)S(1)} copy-done((bf16[768,1536]{1,0:T(8,128)(2,1)S(1)}, bf16[768,1536]{1,0:T(8,128)(2,1)}, u32[]{:S(2)}) %copy-start.7) | copy-done | bytes 2359320
  92.0 2.6 %tokens_parts.1 = (bf16[128,768]{1,0:T(8,128)(2,1)S(1)}, bf16[128,768]{1,0:T(8,128)(2,1)S(1)}, bf16[128,768]{1,0:T(8,128)(2,1)S(1)}, f32[128,768]{1,0:T(8,128)S(1)}) custom-call(s32[3]{0:T(128)S(1)} %pad_add_fusion.where, bf16[4,64,1536]{2,1,0:T(8,128)(2,1)S(1)} %bitcast.20, bf16[4,64,1536]{2,1,0:T(8,128)(2,1)S(1)} %bitcast.21, bf16[768,1536]{1,0:T(8,128)(2,1)S(1)} %copy-done.7), custom_call_target="tpu_custom_call" | custom-call | flops 1207959552 | bytes 6291456 | tf_op jit(solution)/shard_map/tokens_parts/pallas_call | solution.py:62
  94.6 1.9 %collective-permute-start.6 = (bf16[128,768]{1,0:T(8,128)(2,1)S(1)}, bf16[128,768]{1,0:T(8,128)(2,1)S(1)}, u32[]{:S(2)}, u32[]{:S(2)}) collective-permute-start(bf16[128,768]{1,0:T(8,128)(2,1)S(1)} %get-tuple-element.22), channel_id=1, source_target_pairs={{0,1},{1,2},{2,3},{3,4},{4,5},{5,6},{6,7},{7,8},{8,9},{9,10},{10,1... | collective-permute-start | bytes 589832 | tf_op jit(solution)/shard_map/ppermute | solution.py:168
  96.5 4.6 %collective-permute-start.7 = (bf16[128,768]{1,0:T(8,128)(2,1)S(1)}, bf16[128,768]{1,0:T(8,128)(2,1)S(1)}, u32[]{:S(2)}, u32[]{:S(2)}) collective-permute-start(bf16[128,768]{1,0:T(8,128)(2,1)S(1)} %get-tuple-element.23), channel_id=1, source_target_pairs={{0,15},{1,0},{2,1},{3,2},{4,3},{5,4},{6,5},{7,6},{8,7},{9,8},{10,9... | collective-permute-start | bytes 589832 | tf_op jit(solution)/shard_map/ppermute | solution.py:169
  101.1 1.9 %collective-permute-start.11 = (bf16[128,768]{1,0:T(8,128)(2,1)S(1)}, bf16[128,768]{1,0:T(8,128)(2,1)S(1)}, u32[]{:S(2)}, u32[]{:S(2)}) collective-permute-start(bf16[128,768]{1,0:T(8,128)(2,1)S(1)} %get-tuple-element.31), channel_id=1, source_target_pairs={{0,2},{1,3},{2,0},{3,1},{4,6},{5,7},{6,4},{7,5},{8,10},{9,11},{10,... | collective-permute-start | bytes 589832 | tf_op jit(solution)/shard_map/ppermute | solution.py:170
  103.0 2.5 %collective-permute-done.1.refs_4_ = bf16[256,1536]{1,0:T(8,128)(2,1)} collective-permute-done((bf16[256,1536]{1,0:T(8,128)(2,1)S(1)}, bf16[256,1536]{1,0:T(8,128)(2,1)}, u32[]{:S(2)}, u32[]{:S(2)}) %collective-permute-start.1) | collective-permute-done | bytes 786464 | tf_op jit(solution)/shard_map/ppermute | solution.py:157
  105.5 1.9 %collective-permute-start.12 = (bf16[4,2,64,768]{3,2,1,0:T(8,128)(2,1)}, bf16[4,2,64,768]{3,2,1,0:T(8,128)(2,1)}, u32[]{:S(2)}, u32[]{:S(2)}) collective-permute-start(bf16[4,2,64,768]{3,2,1,0:T(8,128)(2,1)} %collective-permute-done.4.refs_3_), channel_id=1, source_target_pairs={{0,128},{128,256},{256,384},{384,0},{1,129},{129,257},{257,385},{3... | collective-permute-start | bytes 2359304 | tf_op jit(solution)/shard_map/ppermute | solution.py:174
  107.5 3.0 %collective-permute-start.10 = (bf16[256,1536]{1,0:T(8,128)(2,1)}, bf16[256,1536]{1,0:T(8,128)(2,1)}, u32[]{:S(2)}, u32[]{:S(2)}) collective-permute-start(bf16[256,1536]{1,0:T(8,128)(2,1)} %collective-permute-done.2.refs_7_), channel_id=1, source_target_pairs={{0,16},{16,0},{32,48},{48,32},{64,80},{80,64},{96,112},{112,96},{1... | collective-permute-start | bytes 2359304 | tf_op jit(solution)/shard_map/ppermute | solution.py:176
  110.5 4.5 %collective-permute-start.8 = (bf16[256,1536]{1,0:T(8,128)(2,1)}, bf16[256,1536]{1,0:T(8,128)(2,1)}, u32[]{:S(2)}, u32[]{:S(2)}) collective-permute-start(bf16[256,1536]{1,0:T(8,128)(2,1)} %collective-permute-done.2.refs_7_), channel_id=1, source_target_pairs={{0,384},{128,0},{256,128},{384,256},{1,385},{129,1},{257,129},{385... | collective-permute-start | bytes 2359304 | tf_op jit(solution)/shard_map/ppermute | solution.py:173
  115.0 2.2 %collective-permute-start.9 = (bf16[256,1536]{1,0:T(8,128)(2,1)}, bf16[256,1536]{1,0:T(8,128)(2,1)}, u32[]{:S(2)}, u32[]{:S(2)}) collective-permute-start(bf16[256,1536]{1,0:T(8,128)(2,1)} %collective-permute-done.1.refs_4_), channel_id=1, source_target_pairs={{0,16},{16,0},{32,48},{48,32},{64,80},{80,64},{96,112},{112,96},{1... | collective-permute-start | bytes 2359304 | tf_op jit(solution)/shard_map/ppermute | solution.py:175
  117.2 0.8 add_convert_fusion.1
  118.0 6.2 %all-to-all-start.1 = ((bf16[4,32,768]{2,1,0:T(8,128)(2,1)}), bf16[4,32,768]{2,1,0:T(8,128)(2,1)S(1)}, u32[]{:S(2)}, u32[]{:S(2)}) async-start(bf16[4,32,768]{2,1,0:T(8,128)(2,1)} %bitcast.9), calls=%async_computation.1 | async-start | bytes 393216 | tf_op jit(solution)/shard_map/all_to_all | solution.py:180
  124.2 1.1 copy-done.1
  125.3 1.1 copy-done.3
  126.5 1.1 copy-done.5
  127.6 6.0 %weight_part.2.refs_3_ = bf16[768,1536]{1,0:T(8,128)(2,1)S(1)} custom-call(s32[3]{0:T(128)S(1)} %pad_add_fusion.where, bf16[4,2,64,768]{3,2,1,0:T(8,128)(2,1)S(1)} %bitcast.19, bf16[256,1536]{1,0:T(8,128)(2,1)S(1)} %copy-done.1, bf16[256,1536]{1,0:T(8,128)(2,1)S(1)} %copy-done.5, bf16[4,2,64,768]{3,2,1,0:T(8,128)(2,1)} %collective-permute-done.4.refs_3_, ...), custom_call_target="tpu_custom_call" | custom-call | tf_op jit(solution)/shard_map/weight_part/pallas_call | solution.py:107
  133.7 3.5 %all-to-all-done.1 = bf16[4,32,768]{2,1,0:T(8,128)(2,1)S(1)} async-done(((bf16[4,32,768]{2,1,0:T(8,128)(2,1)}), bf16[4,32,768]{2,1,0:T(8,128)(2,1)S(1)}, u32[]{:S(2)}, u32[]{:S(2)}) %all-to-all-start.1) | async-done | bytes 196640 | tf_op jit(solution)/shard_map/all_to_all | solution.py:180
  137.2 6.1 %collective-permute-start.13 = (bf16[256,1536]{1,0:T(8,128)(2,1)}, bf16[256,1536]{1,0:T(8,128)(2,1)S(1)}, u32[]{:S(2)}, u32[]{:S(2)}) collective-permute-start(bf16[256,1536]{1,0:T(8,128)(2,1)} %collective-permute-done.8.refs_1_), channel_id=1, source_target_pairs={{0,16},{16,0},{32,48},{48,32},{64,80},{80,64},{96,112},{112,96},{1... | collective-permute-start | bytes 2359304 | tf_op jit(solution)/shard_map/ppermute | solution.py:186
  143.9 1.4 collective-permute-done.13.refs_2_
  145.4 4.5 %weight_part.3 = bf16[768,1536]{1,0:T(8,128)(2,1)} custom-call(s32[3]{0:T(128)S(1)} %pad_add_fusion.where, bf16[4,2,64,768]{3,2,1,0:T(8,128)(2,1)} %collective-permute-done.12.refs_0_, bf16[256,1536]{1,0:T(8,128)(2,1)} %collective-permute-done.8.refs_1_, bf16[256,1536]{1,0:T(8,128)(2,1)S(1)} %collective-permute-done.13.refs_2_, ...), custom_call_target="tpu_custom_call" | custom-call | tf_op jit(solution)/shard_map/weight_part/pallas_call | solution.py:107
  (31 shorter events, 2.0 us)
Async XLA Ops:
  0.6 34.4 %copy-start.6 = (bf16[768,1536]{1,0:T(8,128)(2,1)S(1)}, bf16[768,1536]{1,0:T(8,128)(2,1)}, u32[]{:S(2)}) copy-start(bf16[768,1536]{1,0:T(8,128)(2,1)} %w.1) | copy-start | bytes 7077892
  35.8 11.5 %collective-permute-start = (bf16[256,1536]{1,0:T(8,128)(2,1)S(1)}, bf16[256,1536]{1,0:T(8,128)(2,1)S(1)}, u32[]{:S(2)}, u32[]{:S(2)}) collective-permute-start(bf16[256,1536]{1,0:T(8,128)(2,1)S(1)} %convolution_convert_fusion), channel_id=1, source_target_pairs={{0,16},{16,0},{32,48},{48,32},{64,80},{80,64},{96,112},{112,96},{1... | collective-permute-start | bytes 2359304 | tf_op jit(solution)/shard_map/ppermute | solution.py:141
  49.0 16.2 %copy-start.8 = (bf16[64,1536]{1,0:T(8,128)(2,1)S(1)}, bf16[64,1536]{1,0:T(8,128)(2,1)}, u32[]{:S(2)}) copy-start(bf16[64,1536]{1,0:T(8,128)(2,1)} %param.5) | copy-start | bytes 589828
  49.0 16.0 %all-to-all-start = ((bf16[4,64,1536]{2,1,0:T(8,128)(2,1)}), bf16[4,64,1536]{2,1,0:T(8,128)(2,1)S(1)}, u32[]{:S(2)}, u32[]{:S(2)}) async-start(bf16[4,64,1536]{2,1,0:T(8,128)(2,1)} %bitcast.22), calls=%async_computation | async-start | bytes 1572864 | tf_op jit(solution)/shard_map/all_to_all | solution.py:147
  53.4 36.3 %collective-permute-start.4 = (bf16[4,2,64,768]{3,2,1,0:T(8,128)(2,1)S(1)}, bf16[4,2,64,768]{3,2,1,0:T(8,128)(2,1)}, u32[]{:S(2)}, u32[]{:S(2)}) collective-permute-start(bf16[4,2,64,768]{3,2,1,0:T(8,128)(2,1)S(1)} %bitcast.17), channel_id=1, source_target_pairs={{0,128},{128,256},{256,384},{384,0},{1,129},{129,257},{257,385},{3... | collective-permute-start | bytes 2359304 | tf_op jit(solution)/shard_map/ppermute | solution.py:149
  56.5 33.2 %collective-permute-start.5 = (bf16[4,2,64,768]{3,2,1,0:T(8,128)(2,1)S(1)}, bf16[4,2,64,768]{3,2,1,0:T(8,128)(2,1)S(1)}, u32[]{:S(2)}, u32[]{:S(2)}) collective-permute-start(bf16[4,2,64,768]{3,2,1,0:T(8,128)(2,1)S(1)} %bitcast.18), channel_id=1, source_target_pairs={{0,384},{128,0},{256,128},{384,256},{1,385},{129,1},{257,129},{385... | collective-permute-start | bytes 2359304 | tf_op jit(solution)/shard_map/ppermute | solution.py:150
  76.8 41.2 %copy-start = (bf16[256,1536]{1,0:T(8,128)(2,1)}, bf16[256,1536]{1,0:T(8,128)(2,1)S(1)}, u32[]{:S(2)}) copy-start(bf16[256,1536]{1,0:T(8,128)(2,1)S(1)} %all_gather.7.refs_1_) | copy-start | bytes 2359300
  76.8 12.9 %collective-permute-start.3 = (bf16[256,1536]{1,0:T(8,128)(2,1)S(1)}, bf16[256,1536]{1,0:T(8,128)(2,1)S(1)}, u32[]{:S(2)}, u32[]{:S(2)}) collective-permute-start(bf16[256,1536]{1,0:T(8,128)(2,1)S(1)} %all_gather.7.refs_1_), channel_id=1, source_target_pairs={{0,16},{16,0},{32,48},{48,32},{64,80},{80,64},{96,112},{112,96},{1... | collective-permute-start | bytes 2359304 | tf_op jit(solution)/shard_map/ppermute | solution.py:156
  83.1 22.5 %collective-permute-start.1 = (bf16[256,1536]{1,0:T(8,128)(2,1)S(1)}, bf16[256,1536]{1,0:T(8,128)(2,1)}, u32[]{:S(2)}, u32[]{:S(2)}) collective-permute-start(bf16[256,1536]{1,0:T(8,128)(2,1)S(1)} %all_gather.7.refs_1_), channel_id=1, source_target_pairs={{0,128},{128,256},{256,384},{384,0},{1,129},{129,257},{257,385},{3... | collective-permute-start | bytes 2359304 | tf_op jit(solution)/shard_map/ppermute | solution.py:157
  86.3 21.2 %collective-permute-start.2 = (bf16[256,1536]{1,0:T(8,128)(2,1)S(1)}, bf16[256,1536]{1,0:T(8,128)(2,1)}, u32[]{:S(2)}, u32[]{:S(2)}) collective-permute-start(bf16[256,1536]{1,0:T(8,128)(2,1)S(1)} %all_gather.7.refs_1_), channel_id=1, source_target_pairs={{0,384},{128,0},{256,128},{384,256},{1,385},{129,1},{257,129},{385... | collective-permute-start | bytes 2359304 | tf_op jit(solution)/shard_map/ppermute | solution.py:158
  89.7 28.3 %copy-start.2 = (bf16[4,2,64,768]{3,2,1,0:T(8,128)(2,1)}, bf16[4,2,64,768]{3,2,1,0:T(8,128)(2,1)S(1)}, u32[]{:S(2)}) copy-start(bf16[4,2,64,768]{3,2,1,0:T(8,128)(2,1)S(1)} %collective-permute-done.5.refs_6_) | copy-start | bytes 2359300
  89.7 28.3 %copy-start.4 = (bf16[256,1536]{1,0:T(8,128)(2,1)}, bf16[256,1536]{1,0:T(8,128)(2,1)S(1)}, u32[]{:S(2)}) copy-start(bf16[256,1536]{1,0:T(8,128)(2,1)S(1)} %collective-permute-done.3.refs_2_) | copy-start | bytes 2359300
  89.7 2.2 %copy-start.7 = (bf16[768,1536]{1,0:T(8,128)(2,1)S(1)}, bf16[768,1536]{1,0:T(8,128)(2,1)}, u32[]{:S(2)}) copy-start(bf16[768,1536]{1,0:T(8,128)(2,1)} %w.1) | copy-start | bytes 7077892
  94.6 12.9 %collective-permute-start.6 = (bf16[128,768]{1,0:T(8,128)(2,1)S(1)}, bf16[128,768]{1,0:T(8,128)(2,1)S(1)}, u32[]{:S(2)}, u32[]{:S(2)}) collective-permute-start(bf16[128,768]{1,0:T(8,128)(2,1)S(1)} %get-tuple-element.22), channel_id=1, source_target_pairs={{0,1},{1,2},{2,3},{3,4},{4,5},{5,6},{6,7},{7,8},{8,9},{9,10},{10,1... | collective-permute-start | bytes 589832 | tf_op jit(solution)/shard_map/ppermute | solution.py:168
  96.5 10.9 %collective-permute-start.7 = (bf16[128,768]{1,0:T(8,128)(2,1)S(1)}, bf16[128,768]{1,0:T(8,128)(2,1)S(1)}, u32[]{:S(2)}, u32[]{:S(2)}) collective-permute-start(bf16[128,768]{1,0:T(8,128)(2,1)S(1)} %get-tuple-element.23), channel_id=1, source_target_pairs={{0,15},{1,0},{2,1},{3,2},{4,3},{5,4},{6,5},{7,6},{8,7},{9,8},{10,9... | collective-permute-start | bytes 589832 | tf_op jit(solution)/shard_map/ppermute | solution.py:169
  101.1 16.1 %collective-permute-start.11 = (bf16[128,768]{1,0:T(8,128)(2,1)S(1)}, bf16[128,768]{1,0:T(8,128)(2,1)S(1)}, u32[]{:S(2)}, u32[]{:S(2)}) collective-permute-start(bf16[128,768]{1,0:T(8,128)(2,1)S(1)} %get-tuple-element.31), channel_id=1, source_target_pairs={{0,2},{1,3},{2,0},{3,1},{4,6},{5,7},{6,4},{7,5},{8,10},{9,11},{10,... | collective-permute-start | bytes 589832 | tf_op jit(solution)/shard_map/ppermute | solution.py:170
  105.5 28.1 %collective-permute-start.12 = (bf16[4,2,64,768]{3,2,1,0:T(8,128)(2,1)}, bf16[4,2,64,768]{3,2,1,0:T(8,128)(2,1)}, u32[]{:S(2)}, u32[]{:S(2)}) collective-permute-start(bf16[4,2,64,768]{3,2,1,0:T(8,128)(2,1)} %collective-permute-done.4.refs_3_), channel_id=1, source_target_pairs={{0,128},{128,256},{256,384},{384,0},{1,129},{129,257},{257,385},{3... | collective-permute-start | bytes 2359304 | tf_op jit(solution)/shard_map/ppermute | solution.py:174
  107.5 16.7 %collective-permute-start.10 = (bf16[256,1536]{1,0:T(8,128)(2,1)}, bf16[256,1536]{1,0:T(8,128)(2,1)}, u32[]{:S(2)}, u32[]{:S(2)}) collective-permute-start(bf16[256,1536]{1,0:T(8,128)(2,1)} %collective-permute-done.2.refs_7_), channel_id=1, source_target_pairs={{0,16},{16,0},{32,48},{48,32},{64,80},{80,64},{96,112},{112,96},{1... | collective-permute-start | bytes 2359304 | tf_op jit(solution)/shard_map/ppermute | solution.py:176
  110.5 26.7 %collective-permute-start.8 = (bf16[256,1536]{1,0:T(8,128)(2,1)}, bf16[256,1536]{1,0:T(8,128)(2,1)}, u32[]{:S(2)}, u32[]{:S(2)}) collective-permute-start(bf16[256,1536]{1,0:T(8,128)(2,1)} %collective-permute-done.2.refs_7_), channel_id=1, source_target_pairs={{0,384},{128,0},{256,128},{384,256},{1,385},{129,1},{257,129},{385... | collective-permute-start | bytes 2359304 | tf_op jit(solution)/shard_map/ppermute | solution.py:173
  115.0 9.2 %collective-permute-start.9 = (bf16[256,1536]{1,0:T(8,128)(2,1)}, bf16[256,1536]{1,0:T(8,128)(2,1)}, u32[]{:S(2)}, u32[]{:S(2)}) collective-permute-start(bf16[256,1536]{1,0:T(8,128)(2,1)} %collective-permute-done.1.refs_4_), channel_id=1, source_target_pairs={{0,16},{16,0},{32,48},{48,32},{64,80},{80,64},{96,112},{112,96},{1... | collective-permute-start | bytes 2359304 | tf_op jit(solution)/shard_map/ppermute | solution.py:175
  118.0 19.2 %all-to-all-start.1 = ((bf16[4,32,768]{2,1,0:T(8,128)(2,1)}), bf16[4,32,768]{2,1,0:T(8,128)(2,1)S(1)}, u32[]{:S(2)}, u32[]{:S(2)}) async-start(bf16[4,32,768]{2,1,0:T(8,128)(2,1)} %bitcast.9), calls=%async_computation.1 | async-start | bytes 393216 | tf_op jit(solution)/shard_map/all_to_all | solution.py:180
  124.2 1.1 copy-start.1
  125.3 1.1 copy-start.3
  126.5 1.1 copy-start.5
  137.2 8.2 %collective-permute-start.13 = (bf16[256,1536]{1,0:T(8,128)(2,1)}, bf16[256,1536]{1,0:T(8,128)(2,1)S(1)}, u32[]{:S(2)}, u32[]{:S(2)}) collective-permute-start(bf16[256,1536]{1,0:T(8,128)(2,1)} %collective-permute-done.8.refs_1_), channel_id=1, source_target_pairs={{0,16},{16,0},{32,48},{48,32},{64,80},{80,64},{96,112},{112,96},{1... | collective-permute-start | bytes 2359304 | tf_op jit(solution)/shard_map/ppermute | solution.py:186
